TPU v7x, 32 devices: a whole 2x2x4 slice. The times are simulated.
32 devices in a mesh: rows: 4 (over y, core), seq: 8 (over z, x).
Axes of the slice: x: 2, y: 2, z: 4, core: 2. Of those that a mesh axis runs over, the one named last changes fastest.
Arguments:
- tokens: bfloat16 [8, 4096, 768], P('rows', 'seq'), may hold values from -6 to 6
- doc_starts: int32 [8, 8], P('rows'), may hold values from 0 to 4095, as said below
- norm_gain: float32 [768], replicated, may hold values from 0.5 to 1.5
- in_weight: bfloat16 [768, 3376], replicated, may hold values from -0.21875 to 0.21875
- conv_weight: float32 [4, 1792], replicated, may hold values from -3 to 3
- conv_bias: float32 [1792], replicated, may hold values from -3 to 3
- dt_bias: float32 [48], replicated, may hold values from -1 to 1
- decay_rate: float32 [48], replicated, may hold values from 0.00012207031 to 0.1
- skip_scale: float32 [24], replicated, may hold values from 0.5 to 2
- out_gain: float32 [1536], replicated, may hold values from 0.5 to 1.5
- out_weight: bfloat16 [1536, 768], replicated, may hold values from -0.15625 to 0.15625
- cotangent: bfloat16 [8, 4096, 768], P('rows', 'seq'), may hold values from -6 to 6
Outputs:
- mixed: bfloat16 [8, 4096, 768], P('rows', 'seq')
- tokens_grad: bfloat16 [8, 4096, 768], P('rows', 'seq')
- norm_gain_grad: float32 [768], replicated
- in_weight_grad: float32 [768, 3376], replicated
- conv_weight_grad: float32 [4, 1792], replicated
- conv_bias_grad: float32 [1792], replicated
- dt_bias_grad: float32 [48], replicated
- decay_rate_grad: float32 [48], replicated
- skip_scale_grad: float32 [24], replicated
- out_gain_grad: float32 [1536], replicated
- out_weight_grad: float32 [1536, 768], replicated
Inputs may be any that keep to these rules, and one draw needn't show every extreme that they name: `doc_starts`: per row increasing, the first 0. In one row of each 2 consecutive rows the second lies in positions 1 to 511 and the others in the last 511 positions, the last being 4095; in every other row start k lies within 256 of k * 512.
All inputs are finite; a program needn't handle non-finite values.
Results may differ from a plain program's by a relative error of at most 0.0079.
Values sent between devices are 32-bit elements; how exact they have to be, the bound alone decides.
A program may use at most 384 MiB of HBM per device.

v0:
```python
from functools import partial

import jax
import jax.numpy as jnp
from jax import lax
from jax.sharding import PartitionSpec as P

INNER = 1536
HEADS = 24
HEAD = 64
STATE = 64
KW = 4


EPS = 1e-05
HIGH = lax.Precision.HIGHEST


def shifted(value, axis, steps):
    count = lax.axis_size(axis)
    leading, last = (max(0, -steps), min(count, count - steps))
    return lax.ppermute(value, axis, [(source, source + steps) for source in range(leading, last)])


def carried_in(array, axis, combine, identity, reverse):
    size, mine = (lax.axis_size(axis), lax.axis_index(axis))
    everything = jax.tree.map(lambda part: lax.all_gather(part, axis), array)
    start = jax.tree.map(
        lambda part, zero: jnp.broadcast_to(jnp.asarray(zero, part.dtype), part.shape),
        array,
        identity,
    )

    def lap(k, before):
        at = size - 1 - k if reverse else k
        reached = at > mine if reverse else at < mine
        new = combine(before, jax.tree.map(lambda part: part[at], everything))
        return jax.tree.map(lambda a, b: jnp.where(reached, a, b), new, before)

    return lax.fori_loop(0, size, lap, start)


def rms_scale(values):
    return lax.rsqrt(jnp.mean(values * values, axis=-1, keepdims=True) + EPS)


def doc_index(starts, positions):
    return jnp.sum((starts[..., None, :] <= positions[:, None]).astype(jnp.int32), axis=-1)


def block_out(values, step_sizes, inputs, readers, logsum, labels, carried_state, edge_label):
    positions = jnp.arange(values.shape[0])
    visible = jnp.logical_and(
        positions[:, None] > positions[None, :], labels[:, None] == labels[None, :]
    ).astype(jnp.float32)
    decays = jnp.exp(jnp.minimum(logsum[:, None, :] - logsum[None, :, :], 0.0))
    intersection = jnp.dot(readers, inputs.T, precision=HIGH)
    weights = decays * (visible * intersection)[:, :, None] * step_sizes[None, :, :]
    result = jnp.einsum("tsh,shp->thp", weights, values, precision=HIGH)
    carried = jnp.exp(logsum) * (labels == edge_label).astype(jnp.float32)[:, None]
    reading = jnp.einsum("tn,hnp->thp", readers, carried_state, precision=HIGH)
    return result + carried[:, :, None] * reading


def block_summary(values, step_sizes, inputs, logsum, labels, edge_label):
    final_log = logsum[-1]
    weights_tail = (
        jnp.exp(final_log[None, :] - logsum)
        * (labels == labels[-1]).astype(jnp.float32)[:, None]
        * step_sizes
    )
    local_sum = jnp.einsum("sh,sn,shp->hnp", weights_tail, inputs, values, precision=HIGH)
    passed = jnp.exp(final_log) * (labels[-1] == edge_label).astype(jnp.float32)
    return (passed, local_sum)


def combine(earlier, later):
    return (earlier[0] * later[0], later[0][..., None, None] * earlier[1] + later[1])


def front(extended, step_part, conv_weight, conv_bias, dt_bias, decay_rate, labels, edges):
    length_here = step_part.shape[1]
    conv_out = conv_bias + sum(
        (conv_weight[offset] * extended[:, offset : offset + length_here] for offset in range(KW))
    )
    activated = jax.nn.silu(conv_out)
    values = activated[..., :INNER].reshape(activated.shape[:2] + (HEADS, HEAD))
    pieces = [
        activated[..., INNER + member * STATE : INNER + (member + 1) * STATE] for member in range(4)
    ]
    step_sizes = jax.nn.softplus(step_part + dt_bias)
    ahead_steps = step_sizes[..., :HEADS]
    behind_values = jnp.flip(values, 1)
    behind_steps = jnp.flip(step_sizes[..., HEADS:], 1)
    behind_inputs = jnp.flip(pieces[1], 1)
    behind_readers = jnp.flip(pieces[3], 1)
    ahead_log = jnp.cumsum(-ahead_steps * decay_rate[:HEADS], axis=1)
    behind_log = jnp.cumsum(-behind_steps * decay_rate[HEADS:], axis=1)
    summary = jax.vmap(block_summary)
    ahead_pass, ahead_sum = summary(values, ahead_steps, pieces[0], ahead_log, labels, edges[0])
    behind_pass, behind_sum = summary(
        behind_values, behind_steps, behind_inputs, behind_log, jnp.flip(labels, 1), edges[1]
    )
    parts = (
        values,
        ahead_steps,
        pieces[0],
        pieces[2],
        ahead_log,
        behind_values,
        behind_steps,
        behind_inputs,
        behind_readers,
        behind_log,
    )
    return (parts, (ahead_pass, ahead_sum, behind_pass, behind_sum))


def rear(parts, gate_part, skip_scale, out_gain, ahead_state, behind_state, labels, edges):
    (
        values,
        ahead_steps,
        ahead_inputs,
        ahead_readers,
        ahead_log,
        behind_values,
        behind_steps,
        behind_inputs,
        behind_readers,
        behind_log,
    ) = parts
    output_fn = jax.vmap(block_out)
    ahead = output_fn(
        values, ahead_steps, ahead_inputs, ahead_readers, ahead_log, labels, ahead_state, edges[0]
    )
    behind = output_fn(
        behind_values,
        behind_steps,
        behind_inputs,
        behind_readers,
        behind_log,
        jnp.flip(labels, 1),
        behind_state,
        edges[1],
    )
    combined = ahead + jnp.flip(behind, 1) + skip_scale[:, None] * values
    gated = combined.reshape(values.shape[:2] + (INNER,)) * jax.nn.silu(gate_part)
    return gated * rms_scale(gated) * out_gain


def on_device(
    tokens,
    doc_starts,
    norm_gain,
    in_weight,
    conv_weight,
    conv_bias,
    dt_bias,
    decay_rate,
    skip_scale,
    out_gain,
    out_weight,
    cotangent,
):
    rows_here, length_here, width = tokens.shape
    place = lax.axis_index("seq")
    positions = place * length_here + jnp.arange(length_here, dtype=jnp.int32)
    labels = doc_index(doc_starts, positions)
    edge_ahead = doc_index(doc_starts, place * length_here - 1 + jnp.zeros((1,), jnp.int32))[:, 0]
    edge_behind = doc_index(doc_starts, (place + 1) * length_here + jnp.zeros((1,), jnp.int32))[
        :, 0
    ]
    edges = (edge_ahead, edge_behind)
    source = tokens.astype(jnp.float32)
    scale = rms_scale(source)
    normed_in = source * scale
    rounded = (normed_in * norm_gain).astype(jnp.bfloat16)
    projected = jnp.dot(rounded, in_weight, preferred_element_type=jnp.float32)
    split = 2 * INNER + 4 * STATE
    gate_part = projected[..., :INNER]
    conv_part = projected[..., INNER:split]
    step_part = projected[..., split:]
    rim = shifted(conv_part[:, length_here - (KW - 1) :], "seq", 1)
    extended = jnp.concatenate([rim, conv_part], axis=1)
    front_fn = partial(front, labels=labels, edges=edges)
    (parts, summaries), front_back = jax.vjp(
        front_fn, extended, step_part, conv_weight, conv_bias, dt_bias, decay_rate
    )
    ahead_pass, ahead_sum, behind_pass, behind_sum = summaries
    identity = (jnp.ones_like(ahead_pass), jnp.zeros_like(ahead_sum))
    ahead_state = carried_in((ahead_pass, ahead_sum), "seq", combine, identity, False)[1]
    behind_state = carried_in((behind_pass, behind_sum), "seq", combine, identity, True)[1]
    rear_fn = partial(rear, labels=labels, edges=edges)
    gated, rear_back = jax.vjp(
        rear_fn, parts, gate_part, skip_scale, out_gain, ahead_state, behind_state
    )
    normed_out = gated.astype(jnp.bfloat16)
    branch = jnp.dot(normed_out, out_weight, preferred_element_type=jnp.float32)
    mixed = (source + branch).astype(jnp.bfloat16)
    out_weight_grad = jnp.einsum(
        "rse,rsd->ed", normed_out, cotangent, preferred_element_type=jnp.float32
    )
    d_gated = jnp.einsum("rsd,ed->rse", cotangent, out_weight, preferred_element_type=jnp.float32)
    d_parts, d_gate, skip_grad, out_gain_grad, d_ahead, d_behind = rear_back(d_gated)
    back_ahead = carried_in((ahead_pass, d_ahead), "seq", combine, identity, True)[1]
    back_behind = carried_in((behind_pass, d_behind), "seq", combine, identity, False)[1]
    d_pass_ahead = jnp.sum(back_ahead * ahead_state, axis=(2, 3))
    d_pass_behind = jnp.sum(back_behind * behind_state, axis=(2, 3))
    d_extended, d_step, conv_weight_grad, conv_bias_grad, dt_bias_grad, decay_rate_grad = (
        front_back((d_parts, (d_pass_ahead, back_ahead, d_pass_behind, back_behind)))
    )
    spill = shifted(d_extended[:, : KW - 1], "seq", -1)
    d_main = d_extended[:, KW - 1 :]
    d_conv = jnp.concatenate(
        [d_main[:, : length_here - (KW - 1)], d_main[:, length_here - (KW - 1) :] + spill], axis=1
    )
    d_projected = jnp.concatenate([d_gate, d_conv, d_step], axis=2).astype(jnp.bfloat16)
    in_weight_grad = jnp.einsum(
        "rsd,rsk->dk", rounded, d_projected, preferred_element_type=jnp.float32
    )
    d_rounded = jnp.einsum(
        "rsk,dk->rsd", d_projected, in_weight, preferred_element_type=jnp.float32
    )
    norm_gain_grad = jnp.sum(d_rounded * normed_in, axis=(0, 1))
    d_normed = d_rounded * norm_gain
    d_source = scale * (
        d_normed - normed_in * jnp.mean(d_normed * normed_in, axis=-1, keepdims=True)
    )
    tokens_grad = (cotangent.astype(jnp.float32) + d_source).astype(jnp.bfloat16)
    totals = lax.psum(
        (
            norm_gain_grad,
            in_weight_grad,
            conv_weight_grad,
            conv_bias_grad,
            dt_bias_grad,
            decay_rate_grad,
            skip_grad,
            out_gain_grad,
            out_weight_grad,
        ),
        ("rows", "seq"),
    )
    return (
        mixed,
        tokens_grad,
        totals[0],
        totals[1],
        totals[2],
        totals[3],
        totals[4],
        totals[5],
        totals[6],
        totals[7],
        totals[8],
    )


def solution(mesh):
    placed = (
        P("rows", "seq", None),
        P("rows", None),
        P(),
        P(),
        P(),
        P(),
        P(),
        P(),
        P(),
        P(),
        P(),
        P("rows", "seq", None),
    )
    return jax.shard_map(
        on_device,
        mesh=mesh,
        in_specs=placed,
        out_specs=(
            P("rows", "seq", None),
            P("rows", "seq", None),
            P(),
            P(),
            P(),
            P(),
            P(),
            P(),
            P(),
            P(),
            P(),
        ),
        check_vma=False,
    )
```

profile of v0, /device:TPU:0, one launch (start us, length us, event | category | flops | bytes accessed | tf_op | source)
XLA Modules:
  0.0 1774.1 jit_solution(14861115273005174313)
XLA Ops:
  86.7 12.0 copy.494
  98.9 19.2 %fusion.211 = (f32[2,512,1792]{2,0,1:T(2,128)S(1)}, f32[2,512,1792]{2,0,1:T(2,128)}) fusion(f32[2,512,1792]{2,0,1:T(2,128)} %copy.494, f32[1792]{0:T(1024)} %get-tuple-element.578, f32[2,3,1792]{2,0,1:T(2,128)S(1)} %collective-permute-done, f32[1792]{0:T(1024)} %get-tuple-element.579, f32[1792]{0:T(1024)} %get-tuple-element.577, ...), kind=kLoop, calls=%fused_computation.315 | loop fusion | flops 27525120 | bytes 22098944 | tf_op jit(solution)/shard_map/jvp(jit(silu))/mul | solution.py:86
  203.1 19.6 %all_gather.39 = f32[8,2,24]{2,1,0:T(2,128)S(1)} all-gather(f32[1,2,24]{2,1,0:T(2,128)S(1)} %bitcast_multiply_fusion.12), channel_id=1, replica_groups=mesh['rows'=4,'seq'=8] {'seq'}, dimensions={0}, use_global_device_ids=true | all-gather | bytes 1728 | tf_op jit(solution)/shard_map/all_gather | solution.py:27
  223.4 16.4 all_gather.36
  262.4 79.7 %all-gather.11.cloned.1.call-done = f32[16,24,64,64]{3,2,1,0:T(8,128)} async-done(((f32[2,24,64,64]{3,2,1,0:T(8,128)}), f32[16,24,64,64]{3,2,1,0:T(8,128)}) %all-gather.11.cloned.1.call-update) | async-done | bytes 6291472 | tf_op jit(solution)/shard_map/all_gather | solution.py:27
  342.1 26.2 %while.61 = (s32[]{:T(128)}, f32[2,24,64,64]{3,2,1,0:T(8,128)}, s32[]{:T(128)}, f32[8,2,24]{2,1,0:T(2,128)S(1)}, f32[8,2,24,64,64]{4,3,2,1,0:T(8,128)}, /*index=5*/s32[]{:T(128)}, s32[]{:T(128)}, s32[]{:T(128)}, s32[]{:T(128)}) while((s32[]{:T(128)}, f32[2,24,64,64]{3,2,1,0:T(8,128)}, s32[]{:T(128)}, ...), condition=%wide.region_11.12_spmd.clone, body=%wide.region_10.11_spmd.clone.sunk | while | flops 786440 | bytes 2360047 | solution.py:40
  381.1 58.1 %bitcast_add_fusion.6 = f32[2,512,24,64]{1,3,2,0:T(8,128)} fusion(f32[2,512,24,64]{1,3,2,0:T(8,128)S(1)} %bitcast.299, f32[2,512,24]{1,2,0:T(8,128)S(1)} %copy.418, f32[2,512,24,64]{1,3,2,0:T(8,128)} %rev.41, f32[2,512,24]{1,2,0:T(8,128)S(1)} %copy-done.67, f32[2,512,512]{2,1,0:T(8,128)S(1)} %copy-done.46, f32[2,512,24]{1,2,0:T(8,128)S(1)} %copy-done.65), kind=kOutput, calls=%fused_computation.102 | convolution fusion | flops 9717153792 | bytes 21266432 | tf_op jit(solution)/shard_map/jvp(vmap(tsh,shp->thp))/dot_general | solution.py:59
  449.6 69.9 %all-gather.9.cloned.1.call-done = f32[16,24,64,64]{3,2,1,0:T(8,128)} async-done(((f32[2,24,64,64]{3,2,1,0:T(8,128)}), f32[16,24,64,64]{3,2,1,0:T(8,128)}) %all-gather.9.cloned.1.call-update) | async-done | bytes 6291472 | tf_op jit(solution)/shard_map/all_gather | solution.py:27
  519.6 26.7 %while.60 = (s32[]{:T(128)}, f32[2,24,64,64]{3,2,1,0:T(8,128)}, s32[]{:T(128)}, f32[8,2,24]{2,1,0:T(2,128)S(1)}, f32[8,2,24,64,64]{4,3,2,1,0:T(8,128)}, /*index=5*/s32[]{:T(128)}, s32[]{:T(128)}) while((s32[]{:T(128)}, f32[2,24,64,64]{3,2,1,0:T(8,128)}, s32[]{:T(128)}, f32[8,2,24]{2,1,0:T(2,128)S(1)}, ...), condition=%wide.region_6.7_spmd.clone, body=%wide.region_5.6_spmd.clone.sunk | while | flops 786436 | bytes 2359985 | solution.py:40
  556.4 60.7 %fusion.73 = f32[2,512,24,64]{1,3,2,0:T(8,128)} fusion(f32[2,512,24,64]{1,3,2,0:T(8,128)} %rev.46, f32[2,512,24,64]{1,3,2,0:T(8,128)} %bitcast.294, f32[2,512,24,64]{1,3,2,0:T(8,128)S(1)} %bitcast.301, f32[24]{0:T(128)S(1)} %copy-done.110, f32[2,512,24]{1,2,0:T(8,128)S(1)} %copy-done.59, f32[2,512,24]{1,2,0:T(8,128)S(1)} %copy-done.71, ...), kind=kOutput, calls=%fused_computation.105 | convolution fusion | flops 9721872384 | bytes 27557984 | tf_op jit(solution)/shard_map/jvp(vmap(tsh,shp->thp))/dot_general | solution.py:59
  627.6 12.9 multiply_reduce_fusion.9
  640.8 18.2 %multiply_reduce_fusion.4 = (f32[1536]{0:T(1024)}, f32[2,512]{0,1:T(8,128)S(1)}) fusion(f32[2,512,1536]{2,1,0:T(8,128)} %fusion.122, f32[2,512,1536]{2,0,1:T(2,128)} %get-tuple-element.645, f32[2,512]{0,1:T(8,128)S(1)} %copy.428, f32[1536]{0:T(1024)S(1)} %copy-done.84), kind=kLoop, calls=%fused_computation.106 | loop fusion | flops 9434624 | bytes 12603392 | tf_op jit(solution)/shard_map/transpose(jvp())/reduce_sum | solution.py:148
  659.3 31.6 %multiply_reduce_fusion.5 = (f32[1536]{0:T(1024)}, f32[2,512,1536]{2,0,1:T(2,128)}, bf16[2,512,1536]{2,0,1:T(2,128)(2,1)}, bf16[2,512,1536]{2,0,1:T(2,128)(2,1)}) fusion(f32[2,512,1792]{2,0,1:T(2,128)} %copy-done.7, f32[2,512,1536]{2,0,1:T(2,128)} %copy.496, f32[2,512,1536]{2,0,1:T(2,128)} %get-tuple-element.645, f32[2,512]{0,1:T(8,128)S(1)} %copy.432, ...), kind=kLoop, calls=%fused_computation.107 | loop fusion | flops 36174336 | bytes 44060672 | tf_op jit(solution)/shard_map/transpose(jvp())/reduce_sum | solution.py:146
  713.1 75.3 %fusion.52 = (f32[2,512,24]{1,2,0:T(8,128)}, f32[2,512,24]{1,2,0:T(8,128)S(1)}, f32[2,512,24]{1,2,0:T(8,128)}, f32[2,512,512]{2,1,0:T(8,128)}) fusion(f32[2,512,24]{1,2,0:T(8,128)S(1)} %copy-done.69, f32[2,512,512]{2,1,0:T(8,128)} %fusion.129, f32[2,512,24]{1,2,0:T(8,128)S(1)} %copy-done.71, f32[2,24,64,512]{3,2,1,0:T(8,128)} %bitcast.286, ...), kind=kOutput, calls=%fused_computation.65 | convolution fusion | flops 9876987904 | bytes 17268736 | tf_op jit(solution)/shard_map/transpose(jvp(vmap(tsh,shp->thp)))/dot_general | solution.py:59
  820.9 75.1 %fusion.50 = (f32[2,512,24]{1,2,0:T(8,128)}, f32[2,512,24]{1,2,0:T(8,128)S(1)}, f32[2,512,24]{1,2,0:T(8,128)}, f32[2,512,512]{2,1,0:T(8,128)}) fusion(f32[2,512,24]{1,2,0:T(8,128)S(1)} %copy-done.65, f32[2,512,512]{2,1,0:T(8,128)} %fusion.127, f32[2,512,24]{1,2,0:T(8,128)S(1)} %copy-done.67, f32[2,512,24,64]{1,3,2,0:T(8,128)} %rev.41, ...), kind=kOutput, calls=%fused_computation.63 | convolution fusion | flops 9876987904 | bytes 17268736 | tf_op jit(solution)/shard_map/transpose(jvp(vmap(tsh,shp->thp)))/dot_general | solution.py:59
  967.0 44.3 %fusion.10 = f32[2,24,64,512]{3,2,1,0:T(8,128)} fusion(f32[2,24,64,512]{3,2,1,0:T(8,128)} %bitcast.290, f32[2,512,24]{1,2,0:T(8,128)S(1)} %copy-done.72, f32[2,512,512]{2,1,0:T(8,128)S(1)} %copy-done.48, f32[2,512,24]{1,2,0:T(8,128)S(1)} %copy-done.70), kind=kOutput, calls=%fused_computation.24 | convolution fusion | flops 9714008064 | bytes 14876672 | tf_op jit(solution)/shard_map/transpose(jvp(vmap(tsh,shp->thp)))/dot_general | solution.py:59
  1011.3 31.4 %while.63 = (s32[]{:T(128)}, f32[2,24,64,64]{3,2,1,0:T(8,128)}, s32[]{:T(128)}, f32[8,2,24]{2,1,0:T(2,128)}, f32[8,2,24,64,64]{4,3,2,1,0:T(8,128)}, /*index=5*/s32[]{:T(128)}, s32[]{:T(128)}, s32[]{:T(128)}, s32[]{:T(128)}) while((s32[]{:T(128)}, f32[2,24,64,64]{3,2,1,0:T(8,128)}, s32[]{:T(128)}, f32[8,2,24]{2,1,0:T(2,128)}, ...), condition=%wide.region_19.20_spmd.clone, body=%wide.region_18.19_spmd.clone.sunk | while | flops 786440 | bytes 2360047 | solution.py:40
  1055.5 15.4 all-gather.13.cloned.1.call-done
  1070.8 31.4 %while.62 = (s32[]{:T(128)}, f32[2,24,64,64]{3,2,1,0:T(8,128)}, s32[]{:T(128)}, f32[8,2,24]{2,1,0:T(2,128)}, f32[8,2,24,64,64]{4,3,2,1,0:T(8,128)}, /*index=5*/s32[]{:T(128)}, s32[]{:T(128)}) while((s32[]{:T(128)}, f32[2,24,64,64]{3,2,1,0:T(8,128)}, s32[]{:T(128)}, f32[8,2,24]{2,1,0:T(2,128)}, f32[8,2,24,64,64]{4,3,2,1,0:T(8,128)}, ...), condition=%wide.region_17.18_spmd.clone, body=%wide.region_16.17_spmd.clone.sunk | while | flops 786436 | bytes 2359985 | solution.py:40
  1140.2 44.2 %add_bitcast_fusion = f32[2,512,24,64]{1,3,2,0:T(8,128)} fusion(f32[2,24,64,512]{3,2,1,0:T(8,128)} %fusion.54, f32[2,512,24]{1,2,0:T(8,128)S(1)} %copy-done.68, f32[2,512,512]{2,1,0:T(8,128)} %fusion.127, f32[2,512,24]{1,2,0:T(8,128)S(1)} %copy-done.66, f32[2,512,24,64]{1,3,2,0:T(8,128)} %rev.47), kind=kOutput, calls=%fused_computation.110 | convolution fusion | flops 9715580928 | bytes 21168128 | tf_op jit(solution)/shard_map/transpose(jvp(vmap(tsh,shp->thp)))/dot_general | solution.py:59
  1194.9 13.5 fusion.68
  1219.0 14.1 fusion.191
  1235.8 13.9 fusion.189
  1251.4 39.8 %multiply_reduce_fusion.2 = (f32[1792]{0:T(1024)}, f32[1792]{0:T(1024)}, f32[1792]{0:T(1024)}, f32[1792]{0:T(1024)}, f32[1792]{0:T(1024)}, /*index=5*/f32[2,512,1792]{2,0,1:T(2,128)S(1)}) fusion(f32[2,512,1792]{2,0,1:T(2,128)S(1)} %bitcast.298, f32[2,3,1792]{2,0,1:T(2,128)S(1)} %copy-done.62, f32[2,512,1792]{2,0,1:T(2,128)} %get-tuple-element.647, ...), kind=kLoop, calls=%fused_computation.88 | loop fusion | flops 45866240 | bytes 29438976 | tf_op jit(solution)/shard_map/transpose(jvp())/reduce_sum | solution.py:84
  1308.7 11.1 pad_add_fusion
  1319.9 22.3 %fusion.185 = f32[2,512,1,24]{3,2,1,0:T(1,128)S(1)} fusion(f32[2,512,64,24]{2,3,1,0:T(8,128)} %copy.481, f32[2,512,64,1]{2,0,1,3:T(2,128)S(1)} %copy-done.54), kind=kOutput, calls=%fused_computation.229 | convolution fusion | flops 18874368 | bytes 6651904 | tf_op jit(solution)/shard_map/transpose(jvp(vmap(sh,sn,shp->hnp)))/dot_general | solution.py:72
  1367.0 22.5 %fusion.187 = f32[2,512,1,24]{3,2,1,0:T(1,128)S(1)} fusion(f32[2,512,64,24]{2,3,1,0:T(8,128)} %copy.477, f32[2,512,64,1]{2,0,1,3:T(2,128)} %get-tuple-element.681), kind=kOutput, calls=%fused_computation.231 | convolution fusion | flops 18874368 | bytes 6651904 | tf_op jit(solution)/shard_map/transpose(jvp(vmap(sh,sn,shp->hnp)))/dot_general | solution.py:72
  1435.2 31.3 %pad_maximum_fusion.1 = bf16[2,512,3376]{2,0,1:T(2,128)(2,1)} fusion(bf16[2,512,48]{2,0,1:T(2,128)(2,1)S(1)} %get-tuple-element.638, bf16[2,3,1792]{2,0,1:T(2,128)(2,1)S(1)} %fusion.193, bf16[2,509,1792]{2,0,1:T(2,128)(2,1)S(1)} %slice-done.2, bf16[2,512,1536]{2,0,1:T(2,128)(2,1)S(1)} %copy-done.16), kind=kLoop, calls=%fused_computation.93 | loop fusion | flops 27656192 | bytes 13828096 | tf_op jit(solution)/shard_map/concatenate | solution.py:217
  1466.5 17.9 %copy.470 = bf16[2,512,3376]{1,2,0:T(8,128)(2,1)} copy(bf16[2,512,3376]{2,0,1:T(2,128)(2,1)} %pad_maximum_fusion.1) | data formatting | bytes 13828096 | tf_op jit(solution)/shard_map/concatenate | solution.py:217
  1502.7 11.3 fusion.97
  1514.0 43.6 %all-reduce.19 = (f32[768]{0:T(1024)}, f32[4,1792]{1,0:T(4,128)}, f32[1792]{0:T(1024)}, f32[48]{0:T(128)}, f32[48]{0:T(128)}, /*index=5*/f32[24]{0:T(128)}, f32[1536]{0:T(1024)}) all-reduce(f32[768]{0:T(1024)S(1)} %get-tuple-element.574, f32[4,1792]{1,0:T(4,128)S(1)} %pad_add_fusion.4, ...), channel_id=1, replica_groups=mesh['rows'=4,'seq'=8] {'rows','seq'}, use_global_device_ids=true, to_apply=%region_38.39 | all-reduce | flops 11384 | bytes 91072 | tf_op jit(solution)/shard_map/psum | solution.py:230
  1562.6 193.8 %all-reduce.23.cloned.1.call-done = (f32[768,3376]{0,1:T(8,128)}, f32[1536,768]{1,0:T(8,128)}) async-done(((f32[768,3376]{0,1:T(8,128)}, f32[1536,768]{1,0:T(8,128)}), (f32[768,3376]{0,1:T(8,128)}, f32[1536,768]{1,0:T(8,128)})) %all-reduce.23.cloned.1.call-update) | async-done | bytes 15089680 | tf_op jit(solution)/shard_map/psum | solution.py:230
  (497 shorter events, 670.6 us)
Async XLA Ops:
  7.2 233.4 %copy-start = (bf16[1536,768]{1,0:T(8,128)(2,1)S(1)}, bf16[1536,768]{1,0:T(8,128)(2,1)}, u32[]{:S(2)}) copy-start(bf16[1536,768]{1,0:T(8,128)(2,1)} %param.30) | copy-start | bytes 7077892
  7.2 334.9 %all-gather.11.cloned.1.call-start = ((), (), s32[]{:S(2)}) async-start(), calls=%async_computation.1 | async-start | bytes 14155776 | tf_op jit(solution)/shard_map/all_gather | solution.py:27
  9.2 23.9 %copy-start.104 = (s32[2,8]{1,0:T(2,128)S(1)}, s32[2,8]{1,0:T(2,128)}, u32[]{:S(2)}) copy-start(s32[2,8]{1,0:T(2,128)} %param.21) | copy-start | bytes 196
  9.2 26.0 %copy-start.106 = (f32[48]{0:T(128)S(1)}, f32[48]{0:T(128)}, u32[]{:S(2)}) copy-start(f32[48]{0:T(128)} %param.27) | copy-start | bytes 580
  27.0 71.9 %collective-permute-start = (f32[2,3,1792]{2,0,1:T(2,128)}, f32[2,3,1792]{2,0,1:T(2,128)S(1)}, u32[]{:S(2)}, u32[]{:S(2)}) collective-permute-start(f32[2,3,1792]{2,0,1:T(2,128)} %copy.391), channel_id=1, source_target_pairs={{0,1},{1,2},{2,3},{3,4},{4,5},{5,6},{6,7},{8,9},{9,10},{10,11},{11... | collective-permute-start | bytes 129032 | tf_op jit(solution)/shard_map/ppermute | solution.py:22
  33.2 224.7 %copy-start.63 = (s32[2,512]{1,0:T(2,128)}, s32[2,512]{1,0:T(2,128)S(1)}, u32[]{:S(2)}) copy-start(s32[2,512]{1,0:T(2,128)S(1)} %convert_reduce_fusion) | copy-start | bytes 12292
  39.5 38.7 %copy-start.11 = (f32[2,512,48]{2,0,1:T(2,128)}, f32[2,512,48]{2,0,1:T(2,128)S(1)}, u32[]{:S(2)}) copy-start(f32[2,512,48]{2,0,1:T(2,128)S(1)} %compare_select_fusion.2) | copy-start | bytes 589828
  58.0 124.7 %copy-start.13 = (f32[2,512,24]{2,0,1:T(2,128)}, f32[2,512,24]{2,0,1:T(2,128)S(1)}, u32[]{:S(2)}) copy-start(f32[2,512,24]{2,0,1:T(2,128)S(1)} %get-tuple-element.671) | copy-start | bytes 294916
  98.9 56.4 %copy-start.55 = (f32[2,512,24]{1,2,0:T(8,128)}, f32[2,512,24]{1,2,0:T(8,128)S(1)}, u32[]{:S(2)}) copy-start(f32[2,512,24]{1,2,0:T(8,128)S(1)} %copy.422) | copy-start | bytes 294916
  123.9 28.3 %copy-start.24 = (f32[2,512,64]{2,0,1:T(2,128)}, f32[2,512,64]{2,0,1:T(2,128)S(1)}, u32[]{:S(2)}) copy-start(f32[2,512,64]{2,0,1:T(2,128)S(1)} %get-tuple-element.655) | copy-start | bytes 786436
  165.2 354.3 %all-gather.9.cloned.1.call-start = ((), (), s32[]{:S(2)}) async-start(), calls=%async_computation | async-start | bytes 14155776 | tf_op jit(solution)/shard_map/all_gather | solution.py:27
  176.2 835.1 %all-gather.15.cloned.1.call-start = ((), (), s32[]{:S(2)}) async-start(), calls=%async_computation.3 | async-start | bytes 14155776 | tf_op jit(solution)/shard_map/all_gather | solution.py:27
  203.0 36.8 %copy-start.98 = (f32[2]{0:T(128)}, f32[2]{0:T(128)S(1)}, u32[]{:S(2)}) copy-start(f32[2]{0:T(128)S(1)} %get-tuple-element.583) | copy-start | bytes 28
  342.1 29.3 %copy-start.36 = (f32[2,512,64]{1,2,0:T(8,128)S(1)}, f32[2,512,64]{1,2,0:T(8,128)}, u32[]{:S(2)}) copy-start(f32[2,512,64]{1,2,0:T(8,128)} %copy.414) | copy-start | bytes 786436
  368.4 70.8 %copy-start.79 = (f32[8,2,24]{2,1,0:T(2,128)}, f32[8,2,24]{2,1,0:T(2,128)S(1)}, u32[]{:S(2)}) copy-start(f32[8,2,24]{2,1,0:T(2,128)S(1)} %get-tuple-element.945) | copy-start | bytes 4612
  519.6 29.8 %copy-start.38 = (f32[2,512,64]{1,2,0:T(8,128)S(1)}, f32[2,512,64]{1,2,0:T(8,128)}, u32[]{:S(2)}) copy-start(f32[2,512,64]{1,2,0:T(8,128)} %copy.399) | copy-start | bytes 786436
  546.3 70.8 %copy-start.80 = (f32[8,2,24]{2,1,0:T(2,128)}, f32[8,2,24]{2,1,0:T(2,128)S(1)}, u32[]{:S(2)}) copy-start(f32[8,2,24]{2,1,0:T(2,128)S(1)} %get-tuple-element.946) | copy-start | bytes 4612
  556.4 60.7 %copy-start.10 = (f32[2,512,1536]{1,2,0}, f32[2,512,1536]{1,2,0:S(1)}, u32[]{:S(2)}) copy-start(f32[2,512,1536]{1,2,0:S(1)} %fusion.224) | copy-start | bytes 18874372
  713.1 357.8 %all-gather.13.cloned.1.call-start = ((), (), s32[]{:S(2)}) async-start(), calls=%async_computation.2 | async-start | bytes 14155776 | tf_op jit(solution)/shard_map/all_gather | solution.py:27
  896.1 860.2 %all-reduce.23.cloned.1.call-start = ((), (), s32[]{:S(2)}) async-start(), calls=%async_computation.4 | async-start | bytes 30179328 | tf_op jit(solution)/shard_map/psum | solution.py:230
  1251.3 39.9 %copy-start.73 = (f32[1792]{0:T(1024)S(1)}, f32[1792]{0:T(1024)}, u32[]{:S(2)}) copy-start(f32[1792]{0:T(1024)} %get-tuple-element.576) | copy-start | bytes 21508
  1251.3 39.9 %copy-start.74 = (f32[1792]{0:T(1024)S(1)}, f32[1792]{0:T(1024)}, u32[]{:S(2)}) copy-start(f32[1792]{0:T(1024)} %get-tuple-element.577) | copy-start | bytes 21508
  1251.4 39.8 %copy-start.75 = (f32[1792]{0:T(1024)S(1)}, f32[1792]{0:T(1024)}, u32[]{:S(2)}) copy-start(f32[1792]{0:T(1024)} %get-tuple-element.578) | copy-start | bytes 21508
  1251.4 39.8 %copy-start.76 = (f32[1792]{0:T(1024)S(1)}, f32[1792]{0:T(1024)}, u32[]{:S(2)}) copy-start(f32[1792]{0:T(1024)} %get-tuple-element.579) | copy-start | bytes 21508
  1319.9 30.3 %copy-start.101 = (f32[2]{0:T(128)S(1)}, f32[2]{0:T(128)}, u32[]{:S(2)}) copy-start(f32[2]{0:T(128)} %copy-done.100) | copy-start | bytes 28
  1367.0 22.5 %copy-start.18 = (f32[2,24,4,128]{1,0,3,2:T(2,128)S(1)}, f32[2,24,4,128]{1,0,3,2:T(2,128)}, u32[]{:S(2)}) copy-start(f32[2,24,4,128]{1,0,3,2:T(2,128)} %copy.411) | copy-start | bytes 294916
  1367.0 22.5 %copy-start.34 = (f32[2,512]{0,1:T(8,128)S(1)}, f32[2,512]{0,1:T(8,128)}, u32[]{:S(2)}) copy-start(f32[2,512]{0,1:T(8,128)} %copy.421) | copy-start | bytes 12292
  1367.0 22.6 %copy-start.50 = (f32[2,512,24]{2,0,1:T(2,128)S(1)}, f32[2,512,24]{2,0,1:T(2,128)}, u32[]{:S(2)}) copy-start(f32[2,512,24]{2,0,1:T(2,128)} %copy.455) | copy-start | bytes 294916
  1367.0 22.6 %copy-start.51 = (f32[2,512,24]{2,0,1:T(2,128)S(1)}, f32[2,512,24]{2,0,1:T(2,128)}, u32[]{:S(2)}) copy-start(f32[2,512,24]{2,0,1:T(2,128)} %copy.454) | copy-start | bytes 294916
  1367.0 22.6 %copy-start.95 = (f32[2,24]{1,0:T(2,128)S(1)}, f32[2,24]{1,0:T(2,128)}, u32[]{:S(2)}) copy-start(f32[2,24]{1,0:T(2,128)} %copy-done.94) | copy-start | bytes 580
  1367.0 30.5 %copy-start.99 = (f32[2]{0:T(128)S(1)}, f32[2]{0:T(128)}, u32[]{:S(2)}) copy-start(f32[2]{0:T(128)} %copy-done.98) | copy-start | bytes 28
  1425.7 6.4 collective-permute-start.1
  (90 other events, 1014.1 us)
Sparse Core Ops, SparseCore 0:
  165.4 176.7 all-gather.10
  344.9 174.6 all-gather.8
  713.2 174.5 all-gather.14
  896.2 174.6 all-gather.12
  1495.4 260.8 all-reduce.22
where the time goes:
time: 1780 us; the launch traced here: 1770 us
  matrix products  614 us (34%)
  other arithmetic  386 us (22%)
  waiting for transfers between devices  359 us (20%)
  local copies, waits for them, and re-layouts  314 us (18%)
  blocking collectives  79.5 us (4%)
    dot_general x6, matrix products, block_out(): result = jnp.einsum('tsh,shp->thp', weights, values, precision=HIGH)  358 us
    psum x1, waiting for transfers between devices, on_device(): lax.psum((norm_gain_grad, in_weight_grad, conv_weight_grad, conv_bias_gra...  194 us
    all_gather x4, waiting for transfers between devices, carried_in(): everything = jax.tree.map(lambda part: lax.all_gather(part, axis), array)  165 us
    dot_general x10, matrix products, block_summary(): jnp.einsum('sh,sn,shp->hnp', weights_tail, inputs, values, precision=HIGH)  133 us
    select_n x32, other arithmetic, lap(): return jax.tree.map(lambda a, b: jnp.where(reached, a, b), new, before)  105 us
    unnamed x233, local copies, waits for them, and re-layouts  56.9 us
    psum x1, blocking collectives, on_device(): lax.psum((norm_gain_grad, in_weight_grad, conv_weight_grad, conv_bias_gra...  43.6 us
    reduce_sum x1, other arithmetic, front(): conv_weight[offset] * extended[:, offset:offset + length_here]  39.8 us
  transfers between devices with their start and end apart: 7, of which 4 were waited for; matrix products, arithmetic and copies ran while one was open for 34% of the time, Pallas kernels for 0%

commit v1 on v0

v1 whole, which is shorter than its diff:
```python
import jax
import jax.numpy as jnp
from jax import lax
from jax.experimental import pallas as pl
from jax.experimental.pallas import tpu as pltpu
from jax.sharding import PartitionSpec as P

D = 768
INNER = 1536
HEADS = 24
HEAD = 64
STATE = 64
KW = 4
EPS = 1e-05

C = 256
GC = 256
G = INNER // GC
HG = GC // HEAD
CONV = INNER + 4 * STATE
PAD = 16
LOG2E = 1.4426950408889634
F32, BF16 = jnp.float32, jnp.bfloat16
NN, NT, TN = ((1,), (0,)), ((1,), (1,)), ((0,), (0,))
MESH = pl.DeviceIdType.MESH
VMEM_LIMIT = 60 * 1024 * 1024


def mm(a, b, dims=NN):
    return lax.dot_general(a, b, (dims, ((), ())), preferred_element_type=F32)


def split2(a):
    hi = a.astype(BF16)
    return hi, (a - hi.astype(F32)).astype(BF16)


def split3(a):
    hi = a.astype(BF16)
    rest = a - hi.astype(F32)
    mid = rest.astype(BF16)
    return hi, mid, (rest - mid.astype(F32)).astype(BF16)


def mm2(a, b, dims=NN):
    hi, lo = split2(a)
    return mm(hi, b, dims) + mm(lo, b, dims)


def mm3(a, b, dims=NN):
    hi, mid, lo = split3(a)
    return mm(hi, b, dims) + mm(mid, b, dims) + mm(lo, b, dims)


def mm22(a, b, dims=NN):
    ahi, alo = split2(a)
    bhi, blo = split2(b)
    return mm(ahi, bhi, dims) + mm(alo, bhi, dims) + mm(ahi, blo, dims)


def sigmoid(x):
    return 1.0 / (1.0 + jnp.exp(-x))


def softplus(x):
    return jnp.maximum(x, 0.0) + jnp.log1p(jnp.exp(-jnp.abs(x)))


def iota(shape, dim):
    return lax.broadcasted_iota(jnp.int32, shape, dim)


def cols(g, width=GC):
    return pl.ds(pl.multiple_of(g * width, width), width)


class Exchange:
    def __init__(self, n, rows, chunks, x_ref, y_ref, passes, scratch):
        self.n, self.rows, self.chunks = n, rows, chunks
        self.x, self.y, self.passes = x_ref, y_ref, passes
        (self.st, self.rp, self.qs, self.qr, self.pm, self.pp) = scratch[:6]
        (self.ps, self.pr, self.as_, self.ar, self.bs, self.br) = scratch[6:]
        self.me = lax.axis_index("seq")
        self.partner = self.me + 1 - 2 * (self.me % 2)
        self.has_before = self.me >= 2
        self.has_after = self.me < n - 2

    @staticmethod
    def scratch(rows):
        state = pltpu.VMEM((G, 2, rows, STATE, GC), F32)
        small = pltpu.VMEM((8, INNER), F32)
        dma = pltpu.SemaphoreType.DMA
        return [
            state, state, state, state, small, small,
            dma((1,)), dma((1,)), dma((G,)), dma((G,)), dma((2, G)), dma((2, G)),
        ]

    def greet(self):
        barrier = pltpu.get_barrier_semaphore()

        def hello(to):
            pl.semaphore_signal(barrier, inc=1, device_id={"seq": to}, device_id_type=MESH)

        @pl.when(jnp.logical_not(self.has_before))
        def _():
            self.qr[:, 0] = jnp.zeros_like(self.qr[:, 0])

        @pl.when(jnp.logical_not(self.has_after))
        def _():
            self.qr[:, 1] = jnp.zeros_like(self.qr[:, 1])

        hello(self.partner)
        pl.when(self.has_before)(lambda: hello(self.me - 2))
        pl.when(self.has_after)(lambda: hello(self.me + 2))

    def met(self):
        peers = 1 + self.has_before.astype(jnp.int32) + self.has_after.astype(jnp.int32)
        pl.semaphore_wait(pltpu.get_barrier_semaphore(), peers)

    def pass_copy(self):
        return pltpu.make_async_remote_copy(
            self.pm, self.pp, self.ps.at[0], self.pr.at[0],
            device_id={"seq": self.partner}, device_id_type=MESH)

    def pair_copy(self, g):
        return pltpu.make_async_remote_copy(
            self.st.at[g], self.rp.at[g], self.as_.at[g], self.ar.at[g],
            device_id={"seq": self.partner}, device_id_type=MESH)

    def chain_copy(self, d, g):
        return pltpu.make_async_remote_copy(
            self.qs.at[g, d], self.qr.at[g, d], self.bs.at[d, g], self.br.at[d, g],
            device_id={"seq": self.me + 2 if d == 0 else self.me - 2}, device_id_type=MESH)

    def order(self, d):
        return range(self.chunks) if d == 0 else range(self.chunks - 1, -1, -1)

    def passing(self, d, b, where):
        row = 8 * self.passes[d] + b
        return self.p_ref[row : row + 1, where]

    def set_passes(self, p_ref):
        self.p_ref = p_ref

    def totals_of_passes(self):
        self.pm[...] = jnp.zeros_like(self.pm)
        for d in range(2):
            for r in range(self.rows):
                total = None
                for c in self.order(d):
                    one = self.passing(d, r * self.chunks + c, slice(None))
                    total = one if total is None else total * one
                self.pm[d * self.rows + r : d * self.rows + r + 1, :] = total

    def totals(self, g):
        for d in range(2):
            for r in range(self.rows):
                total = None
                for c in self.order(d):
                    b = r * self.chunks + c
                    one = self.x[b, d, :, cols(g)]
                    total = one if total is None else self.passing(d, b, cols(g)) * total + one
                self.st[g, d, r] = total

    def chain(self, d, g):
        has_in, has_out = (
            (self.has_before, self.has_after) if d == 0 else (self.has_after, self.has_before))
        copy = self.chain_copy(d, g)
        pl.when(has_in)(copy.wait_recv)
        first = self.me % 2 == d
        for r in range(self.rows):
            row = d * self.rows + r
            mine, theirs = self.st[g, d, r], self.rp[g, d, r]
            p_mine = self.pm[row : row + 1, cols(g)]
            p_theirs = self.pp[row : row + 1, cols(g)]
            before = self.qr[g, d, r]
            middle = jnp.where(first, p_mine, p_theirs) * before + jnp.where(first, mine, theirs)
            self.qs[g, d, r] = (
                jnp.where(first, p_theirs, p_mine) * middle + jnp.where(first, theirs, mine))
            state = jnp.where(first, before, middle)
            order = list(self.order(d))
            for i, c in enumerate(order):
                b = r * self.chunks + c
                self.y[b, d, :, cols(g)] = state
                if i < len(order) - 1:
                    state = (
                        self.passing(d, b, cols(g)) * state + self.x[b, d, :, cols(g)])
        pl.when(has_out)(copy.start)

    def advance(self, step):
        late = self.n // 2 - 1
        place = self.me // 2

        @pl.when(jnp.logical_and(step >= 1, step < G + 1))
        def _():
            self.pair_copy(step - 1).wait_recv()

        @pl.when(step == 1)
        def _():
            self.pass_copy().wait_recv()

        for d in range(2):
            g = step - 1 - (place if d == 0 else late - place)
            pl.when(jnp.logical_and(g >= 0, g < G))(lambda d=d, g=g: self.chain(d, g))

    def steps(self):
        return G + self.n // 2

    def finish(self):
        self.pass_copy().wait_send()

        @pl.loop(0, G)
        def _(g):
            self.pair_copy(g).wait_send()
            pl.when(self.has_after)(self.chain_copy(0, g).wait_send)
            pl.when(self.has_before)(self.chain_copy(1, g).wait_send)


def pieces(x):
    return [x[:, i * STATE : (i + 1) * STATE] for i in range(4)]


def front_kernel(
    n, rows, length,
    tok, halo, ngain, w, wst, cw, cb, dtb, rate, skip, mask, labcol, sel,
    rounded_o, c_o, p_o, xact_o, y_o, rows_o, q_o, q2_o, pexp_o, sin_o,
    rext, vhi, vlo, gc, sloc, *scratch,
):
    k = pl.program_id(0)
    chunks = length // C
    blocks = rows * chunks
    ex = Exchange(n, rows, chunks, sloc, sin_o, (0, 1), scratch)
    ex.set_passes(pexp_o)

    def convolved(r):
        p = mm(rext[r], w[...])
        p_o[r] = p
        first = PAD - (KW - 1)
        out = cb[...]
        for i in range(KW):
            out = out + cw[i : i + 1, :] * p[first + i : first + i + length]
        c_o[r * length : (r + 1) * length, :] = out
        return out * sigmoid(out)

    @pl.when(k == 0)
    def _():
        ex.greet()
        for r in range(rows):
            here = slice(r * length, (r + 1) * length)
            source = tok[here, :].astype(F32)
            for part, at in ((halo[r], slice(0, PAD)), (source, slice(PAD, PAD + length))):
                scale = lax.rsqrt(jnp.mean(part * part, axis=-1, keepdims=True) + EPS)
                rext[r, at, :] = (part * scale * ngain[...]).astype(BF16)
            rounded_o[here, :] = rext[r, PAD:, :]
            xact_o[here, :] = convolved(r)
        upto = (iota((C, C), 0) <= iota((C, C), 1)).astype(BF16)
        t_id, s_id = iota((C, C), 0), iota((C, C), 1)
        for b in range(blocks):
            here = slice(b * C, (b + 1) * C)
            raw = mm(wst[...], rounded_o[here, :], NT)
            step = softplus(raw + dtb[...])
            log = -LOG2E * rate[...] * step
            total = mm3(log, upto)
            size = jnp.log(step) * LOG2E
            lf, rc = total[:HEADS], total[HEADS:] - log[HEADS:]
            end_f, end_r = total[:HEADS, C - 1 : C], total[HEADS:, C - 1 : C]
            sf, sr = lf - size[:HEADS], rc + size[HEADS:]
            m = mask[b]
            e_f = jnp.exp2(lf) * m[0:1]
            w_f = jnp.exp2(end_f - lf) * step[:HEADS] * m[1:2]
            e_r = jnp.exp2(end_r - rc) * m[2:3]
            w_r = jnp.exp2(rc) * step[HEADS:] * m[3:4]
            none = jnp.zeros((32, C), F32)
            rows_o[b] = jnp.concatenate([step, lf, rc, sf, sr, raw], axis=0)
            q = jnp.concatenate([e_f, w_f, e_r, w_r, none], axis=0).T
            q_o[b] = q
            q2_o[b] = jnp.concatenate([lf, rc, sf, sr, none], axis=0).T
            pexp_o[b : b + 1, :] = mm3(q[C - 8 :], sel[0])[7:8]
            pexp_o[8 + b : 9 + b, :] = mm3(q[:8], sel[2])[0:1]
            in_f, in_r, rd_f, rd_r = pieces(xact_o[here, :])
            gf, gr = mm22(rd_f, in_f, NT), mm22(rd_r, in_r, NT)
            same = jnp.logical_and(labcol[b] == m[6:7], t_id != s_id)
            gc[b] = jnp.where(same, jnp.where(t_id > s_id, gf, gr), 0.0)
        ex.totals_of_passes()

    @pl.when(jnp.logical_and(k >= 1, k <= G))
    def _():
        g = k - 1
        for r in range(rows):
            v = convolved(r)
            hi, lo = split2(v)
            vhi[g, r * length : (r + 1) * length, :] = hi
            vlo[g, r * length : (r + 1) * length, :] = lo
            for c in range(chunks):
                b = r * chunks + c
                vb = v[c * C : (c + 1) * C]
                x = xact_o[b * C : (b + 1) * C, :].astype(BF16)
                for d in range(2):
                    scale = mm2(q_o[b], sel[2 * d + 1, :, cols(g)])
                    sloc[b, d, :, cols(g)] = mm(
                        x[:, d * STATE : (d + 1) * STATE], (scale * vb).astype(BF16), TN)
        ex.totals(g)

        @pl.when(g == 0)
        def _():
            ex.met()
            ex.pass_copy().start()

        ex.pair_copy(g).start()

    @pl.when(k > 0)
    def _():
        ex.advance(k - 1)

    @pl.when(jnp.logical_and(k > G, k <= 2 * G))
    def _():
        g = k - 1 - G
        later = iota((C, C), 0) > iota((C, C), 1)
        low = iota((C, 128), 1) < HEAD
        for b in range(blocks):
            here = slice(b * C, (b + 1) * C)
            q2 = pltpu.roll(q2_o[b], 128 - HG * g, 1)
            for pair in range(HG // 2):
                at = slice(pair * 128, (pair + 1) * 128)
                v2 = jnp.concatenate([vhi[g, here, at], vlo[g, here, at]], axis=1)
                outs = []
                for h in (2 * pair, 2 * pair + 1):
                    lt, rt = q2[:, h : h + 1], q2[:, HEADS + h : HEADS + h + 1]
                    ls = rows_o[b, pl.ds(96 + HG * g + h, 1), :]
                    rs = rows_o[b, pl.ds(96 + HEADS + HG * g + h, 1), :]
                    x = jnp.exp2(jnp.where(later, lt - ls, rs - rt))
                    o = mm((gc[b] * x).astype(BF16), v2)
                    outs.append(o[:, :128] + o[:, 128:])
                v = vhi[g, here, at].astype(F32) + vlo[g, here, at].astype(F32)
                y_o[here, at] = jnp.where(low, outs[0], outs[1]) + skip[:, at] * v

    @pl.when(k == pl.num_programs(0) - 1)
    def _():
        ex.finish()


def middle_kernel(
    y, rounded, tok, cot, q, xact, sin, wg, wo, ogain, sel,
    mixed_o, dy_o, dgate_o, ds_o, dread_o, dq_o, wo_grad, ogain_grad, wg_grad,
):
    k = pl.program_id(0)
    x = xact[...].astype(BF16)
    rd_f, rd_r = x[:, 2 * STATE : 3 * STATE], x[:, 3 * STATE :]
    s_f, s_r = sin[0, 0].astype(BF16), sin[0, 1].astype(BF16)
    e_f, e_r = mm2(q[0], sel[0]), mm2(q[0], sel[2])
    r_f, r_r = mm(rd_f, s_f), mm(rd_r, s_r)
    yv = y[...] + e_f * r_f + e_r * r_r
    gate = mm(rounded[...], wg[...])
    sg = sigmoid(gate)
    silu = gate * sg
    gated = yv * silu
    scale = lax.rsqrt(jnp.mean(gated * gated, axis=-1, keepdims=True) + EPS)
    normed = gated * scale
    out = (normed * ogain[...]).astype(BF16)
    mixed_o[...] = (tok[...].astype(F32) + mm(out, wo[...])).astype(BF16)
    dout = mm(cot[...], wo[...], NT)
    go = jnp.sum(dout * normed, axis=0, keepdims=True)
    dn = dout * ogain[...]
    dgated = scale * (dn - normed * jnp.mean(dn * normed, axis=-1, keepdims=True))
    dy = dgated * silu
    dy_o[...] = dy
    dgate = (dgated * yv * sg * (1.0 + gate * (1.0 - sg))).astype(BF16)
    dgate_o[...] = dgate
    u_f, u_r = e_f * dy, e_r * dy
    dq_o[0] = mm2(u_f * r_f, sel[0], NT) + mm2(u_r * r_r, sel[2], NT)
    u_f, u_r = u_f.astype(BF16), u_r.astype(BF16)
    ds_o[0, 1] = mm(rd_f, u_f, TN)
    ds_o[0, 0] = mm(rd_r, u_r, TN)
    dread_o[...] = jnp.concatenate([mm(u_f, s_f, NT), mm(u_r, s_r, NT)], axis=1)

    @pl.when(k == 0)
    def _():
        wo_grad[...] = mm(out, cot[...], TN)
        wg_grad[...] = mm(rounded[...], dgate, TN)
        ogain_grad[...] = jnp.broadcast_to(go, ogain_grad.shape)

    @pl.when(k > 0)
    def _():
        wo_grad[...] += mm(out, cot[...], TN)
        wg_grad[...] += mm(rounded[...], dgate, TN)
        ogain_grad[...] += go


def back_kernel(
    n, rows, length, far,
    c_i, dy_i, xact, cx, rows_i, q_i, q2_i, pexp, sin, ds, dread, dq_i, mask, labcol, dtb, rate, skip, sel,
    dc_o, draw_o, skip_o, small_o,
    gct, dgt, dvs, dss, dts, dqs, dins, pgs, z, *scratch,
):
    k = pl.program_id(0)
    chunks = length // C
    blocks = rows * chunks
    ex = Exchange(n, rows, chunks, ds, z, (1, 0), scratch)
    ex.set_passes(pexp)
    later = iota((C, C), 1) > iota((C, C), 0)

    @pl.when(k == 0)
    def _():
        ex.greet()
        ex.totals_of_passes()

        @pl.loop(0, G)
        def _(g):
            ex.totals(g)

        ex.met()
        ex.pass_copy().start()

        @pl.loop(0, G)
        def _(g):
            ex.pair_copy(g).start()

        differ = iota((C, C), 0) != iota((C, C), 1)
        for b in range(blocks):
            in_f, in_r, rd_f, rd_r = pieces(xact[b * C : (b + 1) * C, :])
            gf, gr = mm22(in_f, rd_f, NT), mm22(in_r, rd_r, NT)
            same = jnp.logical_and(labcol[b] == mask[b, 6:7], differ)
            gct[b] = jnp.where(same, jnp.where(later, gf, gr), 0.0)
        dgt[...] = jnp.zeros_like(dgt)
        dss[...] = jnp.zeros_like(dss)
        dins[...] = jnp.zeros_like(dins)
        pgs[...] = jnp.zeros_like(pgs)
        dqs[...] = dq_i[...]

    @pl.when(k < G)
    def _():
        g = k
        low = iota((C, 128), 1) < HEAD
        lane = iota((C, 128), 1)
        ones = jnp.ones((8, C), BF16)
        skips = jnp.zeros((1, GC), F32)
        for b in range(blocks):
            here = slice(b * C, (b + 1) * C)
            q2 = pltpu.roll(q2_i[b], 128 - HG * g, 1)
            cv = c_i[here, :]
            v = cv * sigmoid(cv)
            dy = dy_i[here, :]
            skips += jnp.sum(dy * v, axis=0, keepdims=True)
            dyhi, dylo = split2(dy)
            vb = v.astype(BF16)
            for pair in range(HG // 2):
                at = slice(pair * 128, (pair + 1) * 128)
                dy2 = jnp.concatenate([dyhi[:, at], dylo[:, at]], axis=1)
                outs = []
                for i in range(2):
                    h = 2 * pair + i
                    mine = low if i == 0 else jnp.logical_not(low)
                    dyh = jnp.where(mine, dyhi[:, at], jnp.zeros((), BF16))
                    dw = mm(vb[:, at], dyh, NT)
                    lt = rows_i[b, pl.ds(48 + HG * g + h, 1), :]
                    rt = rows_i[b, pl.ds(48 + HEADS + HG * g + h, 1), :]
                    ls, rs = q2[:, 48 + h : 49 + h], q2[:, 72 + h : 73 + h]
                    x = jnp.exp2(jnp.where(later, lt - ls, rs - rt))
                    dwx = dw * x
                    dgt[b] += dwx
                    gb = gct[b]
                    o = mm((gb * x).astype(BF16), dy2)
                    outs.append(o[:, :128] + o[:, 128:])
                    de = dwx * gb
                    de_f = jnp.where(later, de, 0.0).astype(BF16)
                    de_r = jnp.where(later, 0.0, de).astype(BF16)
                    hot_f = (lane == HG * g + h).astype(BF16)
                    hot_r = (lane == HEADS + HG * g + h).astype(BF16)
                    dss[b] += mm(de_f, hot_f) + mm(de_r, hot_r)
                    dts[b, pl.ds(HG * g + h, 1), :] = mm(ones, de_f)[0:1]
                    dts[b, pl.ds(HEADS + HG * g + h, 1), :] = mm(ones, de_r)[0:1]
                dvs[g, here, at] = jnp.where(low, outs[0], outs[1]) + skip[:, at] * dy[:, at]
        skip_o[...] = jnp.broadcast_to(skips, skip_o.shape)

    ex.advance(k)

    @pl.when(jnp.logical_and(k >= far, k < far + G))
    def _():
        g = k - far
        for b in range(blocks):
            here = slice(b * C, (b + 1) * C)
            cv = c_i[here, :]
            sg = sigmoid(cv)
            v = cv * sg
            x = xact[here, :].astype(BF16)
            dv = dvs[g, here, :]
            for d in range(2):
                zf = z[b, 1 - d, :, cols(g)]
                zb = zf.astype(BF16)
                pick = sel[2 * d + 1, :, cols(g)]
                weight = mm2(q_i[b], pick)
                m = mm(x[:, d * STATE : (d + 1) * STATE], zb)
                dv += weight * m
                u = weight * v
                dqs[b] += mm2(u * m, pick, NT)
                at = slice(d * STATE, (d + 1) * STATE)
                dins[b, :, at] += mm(u.astype(BF16), zb, NT)
                pgs[8 * d + b : 8 * d + b + 1, cols(g)] = pexp[
                    8 * d + b : 8 * d + b + 1, cols(g)
                ] * jnp.sum(zf * sin[b, d, :, cols(g)], axis=0, keepdims=True)
            dc_o[here, :] = dv * (sg * (1.0 + cv * (1.0 - sg)))

    @pl.when(k == far + G)
    def _():
        ex.finish()
        differ = iota((C, C), 0) != iota((C, C), 1)
        from_t = (iota((C, C), 0) >= iota((C, C), 1)).astype(BF16)
        after_t = (iota((C, C), 0) > iota((C, C), 1)).astype(BF16)
        pg_f, pg_r = mm22(sel[0].astype(F32), pgs[0:8], NT), mm22(sel[2].astype(F32), pgs[8:16], NT)
        sums = jnp.zeros((2 * HEADS, 128), F32)
        for b in range(blocks):
            here = slice(b * C, (b + 1) * C)
            same = jnp.logical_and(labcol[b] == mask[b, 6:7], differ)
            dg = jnp.where(same, dgt[b], 0.0)
            dg_f = jnp.where(later, dg, 0.0).astype(BF16)
            dg_r = jnp.where(later, 0.0, dg).astype(BF16)
            in_f, in_r, rd_f, rd_r = pieces(xact[here, :].astype(BF16))
            dx = jnp.concatenate(
                [
                    dins[b, :, :STATE] + mm(dg_f, rd_f),
                    dins[b, :, STATE:] + mm(dg_r, rd_r),
                    dread[here, :STATE] + mm(dg_f, in_f, TN),
                    dread[here, STATE:] + mm(dg_r, in_r, TN),
                ],
                axis=1,
            )
            cv = cx[here, :]
            sg = sigmoid(cv)
            dc_o[here, :] = dx * (sg * (1.0 + cv * (1.0 - sg)))
            dq, col, row = dqs[b].T, dss[b].T, dts[b]
            e_f, w_f, e_r, w_r = [dq[i * HEADS : (i + 1) * HEADS] for i in range(4)]
            cs_f, cs_r = col[:HEADS], col[HEADS : 2 * HEADS]
            d_lf = row[:HEADS] - cs_f + e_f - w_f
            d_rc = cs_r - row[HEADS:] - e_r + w_r
            d_size = jnp.concatenate([cs_f + w_f, cs_r + w_r], axis=0)
            end_f = jnp.sum(w_f, axis=1, keepdims=True) + pg_f[:HEADS, b : b + 1]
            end_r = jnp.sum(e_r, axis=1, keepdims=True) + pg_r[2 * HEADS : 3 * HEADS, b : b + 1]
            d_log = jnp.concatenate(
                [mm3(d_lf, from_t) + end_f, mm3(d_rc, after_t) + end_r], axis=0)
            step, raw = rows_i[b, 0:48], rows_i[b, 144:192] + dtb[...]
            sg = sigmoid(raw)
            ratio = jnp.where(raw < -15.0, 1.0, sg / jnp.maximum(step, 1e-30))
            d_raw = -rate[...] * d_log * sg + d_size * ratio
            draw_o[:, here] = d_raw.astype(BF16)
            bias = jnp.sum(d_raw, axis=1, keepdims=True)
            rates = -jnp.sum(step * d_log, axis=1, keepdims=True)
            at = iota((2 * HEADS, 128), 1)
            sums += jnp.where(at == 0, bias, jnp.where(at == 1, rates, 0.0))
        small_o[...] = sums


def last_kernel(
    rows, length,
    dc, halo, p_i, dgate, draw, rounded, tok, cot, ngain, cw, w, wst,
    tg_o, wc_grad, ws_grad, cw_grad, cb_grad, ng_grad,
    acc,
):
    k = pl.program_id(0)
    groups = CONV // GC

    @pl.when(k == 0)
    def _():
        acc[...] = mm(draw[...], wst[...], TN)
        ws_grad[...] = mm(draw[...], rounded[...])

    @pl.when(k < groups)
    def _():
        parts = []
        taps = [jnp.zeros((1, GC), F32) for _ in range(KW)]
        bias = jnp.zeros((1, GC), F32)
        for r in range(rows):
            own = dc[r * length : (r + 1) * length, :]
            ext = jnp.concatenate([own, halo[r]], axis=0)
            total = None
            for i in range(KW):
                one = cw[i : i + 1, :] * ext[KW - 1 - i : KW - 1 - i + length]
                total = one if total is None else total + one
                first = PAD - (KW - 1) + i
                taps[i] += jnp.sum(own * p_i[r, first : first + length, :], axis=0, keepdims=True)
            bias += jnp.sum(own, axis=0, keepdims=True)
            parts.append(total.astype(BF16))
        both = jnp.concatenate(parts, axis=0)
        wc_grad[...] = mm(rounded[...], both, TN)
        acc[...] += mm(both, w[...], NT)
        cw_grad[...] = jnp.concatenate(taps + [jnp.zeros((4, GC), F32)], axis=0)
        cb_grad[...] = jnp.broadcast_to(bias, cb_grad.shape)

    @pl.when(k >= groups)
    def _():
        acc[...] += mm(dgate[...], w[...], NT)

    @pl.when(k == groups + G - 1)
    def _():
        gains = jnp.zeros((1, D), F32)
        for b in range(rows * length // C):
            here = slice(b * C, (b + 1) * C)
            source = tok[here, :].astype(F32)
            scale = lax.rsqrt(jnp.mean(source * source, axis=-1, keepdims=True) + EPS)
            m = source * scale
            d_rounded = acc[here, :]
            gains += jnp.sum(d_rounded * m, axis=0, keepdims=True)
            nn = d_rounded * ngain[...]
            d_source = scale * (nn - m * jnp.mean(nn * m, axis=-1, keepdims=True))
            tg_o[here, :] = (cot[here, :].astype(F32) + d_source).astype(BF16)
        ng_grad[...] = jnp.broadcast_to(gains, ng_grad.shape)


def selectors():
    lane = lax.broadcasted_iota(jnp.int32, (4, 128, INNER), 1)
    kind = lax.broadcasted_iota(jnp.int32, (4, 128, INNER), 0)
    head = lax.broadcasted_iota(jnp.int32, (4, 128, INNER), 2) // HEAD
    return (lane == kind * HEADS + head).astype(BF16)


def shifted(value, axis, steps):
    count = lax.axis_size(axis)
    leading, last = max(0, -steps), min(count, count - steps)
    return lax.ppermute(value, axis, [(i, i + steps) for i in range(leading, last)])


def whole(shape):
    zeros = (0,) * len(shape)
    return pl.BlockSpec(shape, lambda k: zeros)


def struct(shape, dtype=F32):
    return jax.ShapeDtypeStruct(shape, dtype)


def on_device(
    tokens, doc_starts, norm_gain, in_weight, conv_weight, conv_bias, dt_bias, decay_rate,
    skip_scale, out_gain, out_weight, cotangent,
):
    n = lax.axis_size("seq")
    rows, length, _ = tokens.shape
    chunks = length // C
    blocks = rows * chunks
    count = rows * length
    place = lax.axis_index("seq")

    positions = place * length - 1 + jnp.arange(length + 2, dtype=jnp.int32)
    labels = jnp.sum(
        (doc_starts[:, None, :] <= positions[None, :, None]).astype(F32), axis=-1)
    own = labels[:, 1 : length + 1].reshape(blocks, C)
    before = labels[:, :length].reshape(blocks, C)[:, :1]
    after = labels[:, 2:].reshape(blocks, C)[:, C - 1 :]
    mask = jnp.stack(
        [
            (own == before).astype(F32),
            (own == own[:, C - 1 :]).astype(F32),
            (own == after).astype(F32),
            (own == own[:, :1]).astype(F32),
            own, own, own, own,
        ],
        axis=1,
    )
    labcol = own[:, :, None]
    sel = selectors()
    skip = jnp.repeat(skip_scale, HEAD)[None, :]
    wst = in_weight[:, 2 * INNER + 4 * STATE :].T
    cb = conv_bias[None, :]
    dtb, rate = dt_bias[:, None], decay_rate[:, None]
    ngain, ogain = norm_gain[None, :], out_gain[None, :]
    tok, cot = tokens.reshape(count, D), cotangent.reshape(count, D)
    rim = shifted(tokens[:, length - 8 :].astype(F32), "seq", 1)
    keep = (jnp.arange(8) >= 8 - (KW - 1)).astype(F32)[None, :, None]
    halo = jnp.pad(rim * keep, ((0, 0), (PAD - 8, 0), (0, 0)))

    params = dict(vmem_limit_bytes=VMEM_LIMIT)
    dims = ("arbitrary",)

    def col(k):
        return jnp.where(k == 0, G, jnp.minimum(k - 1, G - 1))

    def ycol(k):
        return jnp.clip(k - 1 - G, 0, G - 1)

    front_steps = max(2 * G, G + n // 2) + 1
    rounded, c, p, xact, y, rowsv, q, q2, pexp, sin = pl.pallas_call(
        lambda *refs: front_kernel(n, rows, length, *refs),
        grid=(front_steps,),
        in_specs=[
            whole((count, D)), whole((rows, PAD, D)), whole((1, D)),
            pl.BlockSpec((D, GC), lambda k: (0, G + col(k))),
            whole((2 * HEADS, D)),
            pl.BlockSpec((KW, GC), lambda k: (0, col(k))),
            pl.BlockSpec((1, GC), lambda k: (0, col(k))),
            whole((2 * HEADS, 1)), whole((2 * HEADS, 1)),
            pl.BlockSpec((1, GC), lambda k: (0, ycol(k))),
            whole((blocks, 8, C)), whole((blocks, C, 1)), whole((4, 128, INNER)),
        ],
        out_specs=[
            whole((count, D)),
            pl.BlockSpec((count, GC), lambda k: (0, col(k))),
            pl.BlockSpec((rows, PAD + length, GC), lambda k: (0, 0, col(k))),
            whole((count, GC)),
            pl.BlockSpec((count, GC), lambda k: (0, ycol(k))),
            whole((blocks, 192, C)), whole((blocks, C, 128)), whole((blocks, C, 128)),
            whole((16, INNER)), whole((blocks, 2, STATE, INNER)),
        ],
        out_shape=[
            struct((count, D), BF16), struct((count, CONV)), struct((rows, PAD + length, CONV)),
            struct((count, GC)), struct((count, INNER)), struct((blocks, 192, C)),
            struct((blocks, C, 128)), struct((blocks, C, 128)), struct((16, INNER)),
            struct((blocks, 2, STATE, INNER)),
        ],
        scratch_shapes=[
            pltpu.VMEM((rows, PAD + length, D), BF16),
            pltpu.VMEM((G, count, GC), BF16), pltpu.VMEM((G, count, GC), BF16),
            pltpu.VMEM((blocks, C, C), F32), pltpu.VMEM((blocks, 2, STATE, INNER), F32),
            *Exchange.scratch(rows),
        ],
        compiler_params=pltpu.CompilerParams(
            dimension_semantics=dims, collective_id=0, has_side_effects=True, **params),
        name="front",
    )(tok, halo, ngain, in_weight, wst, conv_weight, cb, dtb, rate, skip, mask, labcol, sel)

    def by_block(shape):
        zeros = (0,) * (len(shape) - 1)
        return pl.BlockSpec(shape, lambda k: (k,) + zeros)

    mixed, dy, dgate, ds, dread, dq, wo_grad, ogain_grad, wg_grad = pl.pallas_call(
        middle_kernel,
        grid=(blocks,),
        in_specs=[
            by_block((C, INNER)), by_block((C, D)), by_block((C, D)), by_block((C, D)),
            by_block((1, C, 128)), by_block((C, GC)), by_block((1, 2, STATE, INNER)),
            whole((D, INNER)), whole((INNER, D)), whole((1, INNER)), whole((4, 128, INNER)),
        ],
        out_specs=[
            by_block((C, D)), by_block((C, INNER)), by_block((C, INNER)),
            by_block((1, 2, STATE, INNER)), by_block((C, 128)), by_block((1, C, 128)),
            whole((INNER, D)), whole((8, INNER)), whole((D, INNER)),
        ],
        out_shape=[
            struct((count, D), BF16), struct((count, INNER)), struct((count, INNER), BF16),
            struct((blocks, 2, STATE, INNER)), struct((count, 128)), struct((blocks, C, 128)),
            struct((INNER, D)), struct((8, INNER)), struct((D, INNER)),
        ],
        compiler_params=pltpu.CompilerParams(dimension_semantics=dims, **params),
        name="middle",
    )(y, rounded, tok, cot, q, xact, sin, in_weight, out_weight, ogain, sel)

    far = max(G, n // 2 + 1)

    def vcol(k):
        return jnp.where(k < far, jnp.minimum(k, G - 1), jnp.minimum(k - far, G - 1))

    def first_pass(k):
        return jnp.minimum(k, G - 1)

    def second_pass(k):
        return jnp.clip(k - far, 0, G)

    dc, draw, skips, small = pl.pallas_call(
        lambda *refs: back_kernel(n, rows, length, far, *refs),
        grid=(far + G + 1,),
        in_specs=[
            pl.BlockSpec((count, GC), lambda k: (0, vcol(k))),
            pl.BlockSpec((count, GC), lambda k: (0, first_pass(k))),
            whole((count, GC)),
            pl.BlockSpec((count, GC), lambda k: (0, G)),
            whole((blocks, 192, C)), whole((blocks, C, 128)), whole((blocks, C, 128)),
            whole((16, INNER)), whole((blocks, 2, STATE, INNER)),
            whole((blocks, 2, STATE, INNER)), whole((count, 128)), whole((blocks, C, 128)),
            whole((blocks, 8, C)), whole((blocks, C, 1)),
            whole((2 * HEADS, 1)), whole((2 * HEADS, 1)),
            pl.BlockSpec((1, GC), lambda k: (0, first_pass(k))),
            whole((4, 128, INNER)),
        ],
        out_specs=[
            pl.BlockSpec((count, GC), lambda k: (0, second_pass(k))),
            whole((2 * HEADS, count)),
            pl.BlockSpec((8, GC), lambda k: (0, first_pass(k))),
            whole((2 * HEADS, 128)),
        ],
        out_shape=[
            struct((count, CONV)), struct((2 * HEADS, count), BF16), struct((8, INNER)),
            struct((2 * HEADS, 128)),
        ],
        scratch_shapes=[
            pltpu.VMEM((blocks, C, C), F32), pltpu.VMEM((blocks, C, C), F32),
            pltpu.VMEM((G, count, GC), F32), pltpu.VMEM((blocks, C, 128), F32),
            pltpu.VMEM((blocks, 2 * HEADS, C), F32), pltpu.VMEM((blocks, C, 128), F32),
            pltpu.VMEM((blocks, C, 128), F32), pltpu.VMEM((16, INNER), F32),
            pltpu.VMEM((blocks, 2, STATE, INNER), F32),
            *Exchange.scratch(rows),
        ],
        compiler_params=pltpu.CompilerParams(
            dimension_semantics=dims, collective_id=1, has_side_effects=True, **params),
        name="back",
    )(c, dy, xact, c, rowsv, q, q2, pexp, sin, ds, dread, dq, mask, labcol, dtb, rate, skip, sel)

    spill = shifted(dc.reshape(rows, length, CONV)[:, :8], "seq", -1)
    groups = CONV // GC

    def conv_col(k):
        return jnp.minimum(k, groups - 1)

    tg, wc_grad, ws_grad, cw_grad, cb_grad, ng_grad = pl.pallas_call(
        lambda *refs: last_kernel(rows, length, *refs),
        grid=(groups + G,),
        in_specs=[
            pl.BlockSpec((count, GC), lambda k: (0, conv_col(k))),
            pl.BlockSpec((rows, 8, GC), lambda k: (0, 0, conv_col(k))),
            pl.BlockSpec((rows, PAD + length, GC), lambda k: (0, 0, conv_col(k))),
            pl.BlockSpec((count, GC), lambda k: (0, jnp.clip(k - groups, 0, G - 1))),
            whole((2 * HEADS, count)), whole((count, D)), whole((count, D)), whole((count, D)),
            whole((1, D)),
            pl.BlockSpec((KW, GC), lambda k: (0, conv_col(k))),
            pl.BlockSpec((D, GC), lambda k: (0, jnp.where(k < groups, G + k, k - groups))),
            whole((2 * HEADS, D)),
        ],
        out_specs=[
            whole((count, D)),
            pl.BlockSpec((D, GC), lambda k: (0, conv_col(k))),
            whole((2 * HEADS, D)),
            pl.BlockSpec((8, GC), lambda k: (0, conv_col(k))),
            pl.BlockSpec((8, GC), lambda k: (0, conv_col(k))),
            whole((8, D)),
        ],
        out_shape=[
            struct((count, D), BF16), struct((D, CONV)), struct((2 * HEADS, D)),
            struct((8, CONV)), struct((8, CONV)), struct((8, D)),
        ],
        scratch_shapes=[pltpu.VMEM((count, D), F32)],
        compiler_params=pltpu.CompilerParams(dimension_semantics=dims, **params),
        name="last",
    )(dc, spill, p, dgate, draw, rounded, tok, cot, ngain, conv_weight, in_weight, wst)

    in_weight_grad = jnp.concatenate([wg_grad, wc_grad, ws_grad.T], axis=1)
    totals = lax.psum(
        (
            ng_grad[0], in_weight_grad, cw_grad[:KW], cb_grad[0], small[:, 0], small[:, 1],
            jnp.sum(skips[0].reshape(HEADS, HEAD), axis=1), ogain_grad[0], wo_grad,
        ),
        ("rows", "seq"),
    )
    return (mixed.reshape(tokens.shape), tg.reshape(tokens.shape)) + totals


def solution(mesh):
    local = P("rows", "seq", None)
    return jax.shard_map(
        on_device,
        mesh=mesh,
        in_specs=(local, P("rows", None)) + (P(),) * 9 + (local,),
        out_specs=(local, local) + (P(),) * 9,
        check_vma=False,
    )
```

time: 1780 us -> 554 us (0.31)
  matrix products: 614 us -> 0 us
  other arithmetic: 386 us -> 12.1 us
  local copies, waits for them, and re-layouts: 314 us -> 38.8 us
  Pallas kernels: 0 us -> 209 us
  waiting for transfers between devices: 359 us -> 222 us
  blocking collectives: 79.5 us -> 41.5 us
    dot_general x32 -> x0, matrix products: 600 us -> none  [the longest x6 358 us: block_out(): result = jnp.einsum('tsh,shp->thp', weights, values, precision=HIGH)]
    pallas_call x0 -> x4, Pallas kernels: none -> 209 us  [the longest x1 74.5 us: on_device(): pl.pallas_call(lambda *refs: front_kernel(n, rows, length, *refs), grid=(...]
    all_gather x4 -> x0, waiting for transfers between devices: 165 us -> none  [carried_in(): everything = jax.tree.map(lambda part: lax.all_gather(part, axis), array)]
    reduce_sum x17 -> x2, other arithmetic: 136 us -> 0.89 us  [the longest x1 0.77 us: on_device(): jnp.sum((doc_starts[:, None, :] <= positions[None, :, None]).astype(F32),...]
    select_n x33 -> x0, other arithmetic: 106 us -> none  [the longest x32 105 us: lap(): return jax.tree.map(lambda a, b: jnp.where(reached, a, b), new, before)]
    rev x15 -> x0, local copies, waits for them, and re-layouts: 57.6 us -> none  [the longest x2 20.8 us: rear(): combined = ahead + jnp.flip(behind, 1) + skip_scale[:, None] * values]
    slice x17 -> x10, local copies, waits for them, and re-layouts: 48.2 us -> 4.74 us  [the longest x1 0.91 us: on_device(): spill = shifted(dc.reshape(rows, length, CONV)[:, :8], 'seq', -1)]
    all_gather x2 -> x0, blocking collectives: 36 us -> none  [carried_in(): everything = jax.tree.map(lambda part: lax.all_gather(part, axis), array)]
  transfers between devices with their start and end apart: 7 -> 3, of which waited for: 4 -> 2; matrix products, arithmetic and copies ran while one was open for 34% -> 4% of each run, Pallas kernels for 0% -> 0%
where the time goes in v1:
time: 554 us; the launch traced here: 545 us
  waiting for transfers between devices  222 us (40%)
  Pallas kernels  209 us (38%)
  blocking collectives  41.5 us (7%)
  local copies, waits for them, and re-layouts  38.8 us (7%)
  between operations  14.7 us (3%)
  other arithmetic  12.1 us (2%)
  starting transfers between devices  6.15 us (1%)
    psum x1, waiting for transfers between devices, on_device(): lax.psum((ng_grad[0], in_weight_grad, cw_grad[:KW], cb_grad[0], small[:,...  217 us
    pallas_call x1, Pallas kernels, on_device(): pl.pallas_call(lambda *refs: front_kernel(n, rows, length, *refs), grid=(...  74.5 us
    pallas_call x1, Pallas kernels, on_device(): pl.pallas_call(lambda *refs: back_kernel(n, rows, length, far, *refs), gr...  66.7 us
    psum x1, blocking collectives, on_device(): lax.psum((ng_grad[0], in_weight_grad, cw_grad[:KW], cb_grad[0], small[:,...  41.5 us
    pallas_call x1, Pallas kernels, on_device(): pl.pallas_call(middle_kernel, grid=(blocks,), in_specs=[by_block((C, INNE...  40.7 us
    pallas_call x1, Pallas kernels, on_device(): pl.pallas_call(lambda *refs: last_kernel(rows, length, *refs), grid=(grou...  27.3 us
    unnamed x21, local copies, waits for them, and re-layouts  25 us
  transfers between devices with their start and end apart: 3, of which 2 were waited for; matrix products, arithmetic and copies ran while one was open for 4% of the time, Pallas kernels for 0%

profile of v1, /device:TPU:0, one launch (start us, length us, event | category | flops | bytes accessed | tf_op | source)
XLA Modules:
  0.0 544.9 jit_solution(11921830835479998147)
XLA Ops:
  7.2 0.7 slice_convert_fusion
  8.0 4.8 collective-permute-start
  12.9 0.8 convert_reduce_fusion
  13.9 1.5 slice_bitcast_fusion.refs_4_.refs_11_
  15.6 1.6 fusion.refs_12_.sel.refs_17_
  17.3 1.1 broadcast_in_dim_reshape.8.refs_11_.refs_13_
  18.5 8.0 %copy.54.refs_3_.wg.refs_10_ = bf16[768,3376]{1,0:T(8,128)(2,1)} copy(bf16[768,3376]{0,1:T(8,128)(2,1)} %param.15) | data formatting | bytes 10371072 | tf_op args[3]
  27.1 0.6 broadcast_in_dim.26.ogain
  27.7 0.6 broadcast_in_dim.22.refs_6_
  28.3 0.7 broadcast_in_dim_reshape.6.refs_9_.refs_16_
  29.0 0.7 copy.55.refs_7_.refs_14_
  29.7 0.7 copy.56.refs_8_.refs_15_
  30.4 0.7 stack.2.refs_10_.refs_12_
  31.2 0.6 pad.4.refs_1_
  31.8 74.5 %front.1 = (bf16[1024,768]{1,0:T(8,128)(2,1)}, f32[1024,1792]{1,0:T(8,128)}, f32[2,528,1792]{2,1,0:T(8,128)}, f32[1024,256]{1,0:T(8,128)}, f32[1024,1536]{1,0:T(...) custom-call(bf16[1024,768]{1,0:T(8,128)(2,1)} %bitcast.10, ...), custom_call_target="tpu_custom_call" | custom-call | tf_op jit(solution)/shard_map/front/pallas_call | solution.py:679
  106.3 40.7 %middle.1 = (bf16[1024,768]{1,0:T(8,128)(2,1)}, f32[1024,1536]{1,0:T(8,128)}, bf16[1024,1536]{1,0:T(8,128)(2,1)}, f32[4,2,64,1536]{3,2,1,0:T(8,128)}, f32[1024,1...) custom-call(f32[1024,1536]{1,0:T(8,128)} %get-tuple-element.40.y, ...), custom_call_target="tpu_custom_call" | custom-call | tf_op jit(solution)/shard_map/middle/pallas_call | solution.py:722
  147.0 66.7 %back.1 = (f32[1024,1792]{1,0:T(8,128)}, bf16[48,1024]{1,0:T(8,128)(2,1)}, f32[8,1536]{1,0:T(8,128)}, f32[48,128]{1,0:T(8,128)}) custom-call(f32[1024,1792]{1,0:T(8,128)} %get-tuple-element.46.refs_0_.refs_3_, f32[1024,1536]{1,0:T(8,128)} %get-tuple-element.47.refs_1_, f32[1024,256]{1,0:T(8,128)} %get-tuple-element.43.xact.refs_2_, ...), custom_call_target="tpu_custom_call" | custom-call | tf_op jit(solution)/shard_map/back/pallas_call | solution.py:755
  213.8 0.9 slice.87
  214.7 1.3 collective-permute-start.1
  215.9 5.4 collective-permute-done.1.refs_1_
  221.3 0.6 copy-done
  222.0 27.3 %last.1 = (bf16[1024,768]{1,0:T(8,128)(2,1)}, f32[768,1792]{1,0:T(8,128)}, f32[48,768]{1,0:T(8,128)}, f32[8,1792]{1,0:T(8,128)}, f32[8,1792]{1,0:T(8,128)}, /*index=5*/f32[8,768]{1,0:T(8,128)}) custom-call(f32[1024,1792]{1,0:T(8,128)} %get-tuple-element.54.refs_0_, f32[2,8,1792]{2,1,0:T(8,128)} %copy-done, f32[2,528,1792]{2,1,0:T(8,128)} %get-tuple-element.55.refs_2_, ...), custom_call_target="tpu_custom_call" | custom-call | tf_op jit(solution)/shard_map/last/pallas_call | solution.py:800
  249.3 1.1 copy.63
  250.4 8.7 %pad_maximum_fusion = f32[768,3376]{1,0:T(8,128)} fusion(f32[768,48]{1,0:T(8,128)S(1)} %copy.63, f32[768,1792]{1,0:T(8,128)} %get-tuple-element.61, f32[768,1536]{1,0:T(8,128)} %get-tuple-element.60), kind=kLoop, calls=%fused_computation | loop fusion | flops 5185536 | bytes 20742144 | tf_op jit(solution)/shard_map/concatenate | solution.py:831
  259.1 0.8 slice_reduce_fusion.4
  260.3 0.8 slice_reduce_fusion.3
  261.2 0.8 slice_reduce_fusion.5
  261.9 0.9 slice_reduce_fusion.2
  262.8 41.5 %all-reduce.1 = (f32[768]{0:T(1024)}, f32[4,1792]{1,0:T(4,128)}, f32[1792]{0:T(1024)}, f32[48]{0:T(128)}, f32[48]{0:T(128)}, /*index=5*/f32[24]{0:T(128)}, f32[1536]{0:T(1024)}) all-reduce(f32[768]{0:T(1024)S(1)} %slice_reduce_fusion.5, f32[4,1792]{1,0:T(4,128)S(1)} %slice.74, ...), channel_id=1, replica_groups=mesh['rows'=4,'seq'=8] {'rows','seq'}, use_global_device_ids=true, to_apply=%region_1.2 | all-reduce | flops 11384 | bytes 91072 | tf_op jit(solution)/shard_map/psum | solution.py:832
  304.3 217.0 %all-reduce.5.cloned.1.call-done = (f32[768,3376]{1,0:T(8,128)}, f32[1536,768]{1,0:T(8,128)}) async-done(((f32[768,3376]{1,0:T(8,128)}, f32[1536,768]{1,0:T(8,128)}), (f32[768,3376]{1,0:T(8,128)}, f32[1536,768]{1,0:T(8,128)})) %all-reduce.5.cloned.1.call-update) | async-done | bytes 15089680 | tf_op jit(solution)/shard_map/psum | solution.py:832
  521.3 11.5 %copy.64 = f32[768,3376]{0,1:T(8,128)} copy(f32[768,3376]{1,0:T(8,128)} %get-tuple-element.124) | data formatting | bytes 20742144
  532.7 4.8 copy.67
  (40 shorter events, 1.7 us)
Async XLA Ops:
  7.2 514.1 %all-reduce.5.cloned.1.call-start = ((), (), s32[]{:S(2)}) async-start(), calls=%async_computation | async-start | bytes 30670848 | tf_op jit(solution)/shard_map/psum | solution.py:832
  8.0 23.1 %collective-permute-start = (f32[2,8,768]{2,1,0:T(8,128)S(1)}, f32[2,8,768]{2,1,0:T(8,128)S(1)}, u32[]{:S(2)}, u32[]{:S(2)}) collective-permute-start(f32[2,8,768]{2,1,0:T(8,128)S(1)} %slice_convert_fusion), channel_id=1, source_target_pairs={{0,1},{1,2},{2,3},{3,4},{4,5},{5,6},{6,7},{8,9},{9,10},{10,11},{11... | collective-permute-start | bytes 147464 | tf_op jit(solution)/shard_map/ppermute | solution.py:618
  18.4 8.0 %copy-start.5 = (f32[768]{0:T(1024)S(1)}, f32[768]{0:T(1024)}, u32[]{:S(2)}) copy-start(f32[768]{0:T(1024)} %param.14) | copy-start | bytes 9220
  18.4 8.6 %copy-start.3 = (f32[1536]{0:T(1024)S(1)}, f32[1536]{0:T(1024)}, u32[]{:S(2)}) copy-start(f32[1536]{0:T(1024)} %param.21) | copy-start | bytes 18436
  18.4 9.2 %copy-start.4 = (f32[1792]{0:T(1024)S(1)}, f32[1792]{0:T(1024)}, u32[]{:S(2)}) copy-start(f32[1792]{0:T(1024)} %param.17) | copy-start | bytes 21508
  18.4 9.8 %copy-start.6 = (f32[24]{0:T(128)S(1)}, f32[24]{0:T(128)}, u32[]{:S(2)}) copy-start(f32[24]{0:T(128)} %param.20) | copy-start | bytes 292
  18.5 10.6 %copy-start.7 = (f32[48]{0:T(128)S(1)}, f32[48]{0:T(128)}, u32[]{:S(2)}) copy-start(f32[48]{0:T(128)} %param.18) | copy-start | bytes 580
  18.5 11.2 %copy-start.8 = (f32[48]{0:T(128)S(1)}, f32[48]{0:T(128)}, u32[]{:S(2)}) copy-start(f32[48]{0:T(128)} %param.19) | copy-start | bytes 580
  214.7 6.7 %collective-permute-start.1 = (f32[2,8,1792]{2,1,0:T(8,128)S(1)}, f32[2,8,1792]{2,1,0:T(8,128)S(1)}, u32[]{:S(2)}, u32[]{:S(2)}) collective-permute-start(f32[2,8,1792]{2,1,0:T(8,128)S(1)} %slice.87), channel_id=1, source_target_pairs={{1,0},{2,1},{3,2},{4,3},{5,4},{6,5},{7,6},{9,8},{10,9},{11,10},{12... | collective-permute-start | bytes 344072 | tf_op jit(solution)/shard_map/ppermute | solution.py:618
  221.3 0.6 copy-start
  259.1 1.1 copy-start.1
  259.1 2.1 copy-start.2
Sparse Core Ops, SparseCore 0:
  259.2 261.9 all-reduce.4

commit v2 on v1

v2 whole, which is shorter than its diff:
```python
import jax
import jax.numpy as jnp
from jax import lax
from jax.experimental import pallas as pl
from jax.experimental.pallas import tpu as pltpu
from jax.sharding import PartitionSpec as P

D = 768
INNER = 1536
HEADS = 24
HEAD = 64
STATE = 64
KW = 4
EPS = 1e-05

C = 256
GC = 256
G = INNER // GC
HG = GC // HEAD
CONV = INNER + 4 * STATE
PAD = 16
LOG2E = 1.4426950408889634
F32, BF16 = jnp.float32, jnp.bfloat16
NN, NT, TN = ((1,), (0,)), ((1,), (1,)), ((0,), (0,))
MESH = pl.DeviceIdType.MESH
VMEM_LIMIT = 60 * 1024 * 1024


def mm(a, b, dims=NN):
    return lax.dot_general(a, b, (dims, ((), ())), preferred_element_type=F32)


def split2(a):
    hi = a.astype(BF16)
    return hi, (a - hi.astype(F32)).astype(BF16)


def split3(a):
    hi = a.astype(BF16)
    rest = a - hi.astype(F32)
    mid = rest.astype(BF16)
    return hi, mid, (rest - mid.astype(F32)).astype(BF16)


def mm2(a, b, dims=NN):
    hi, lo = split2(a)
    return mm(hi, b, dims) + mm(lo, b, dims)


def mm3(a, b, dims=NN):
    hi, mid, lo = split3(a)
    return mm(hi, b, dims) + mm(mid, b, dims) + mm(lo, b, dims)


def mm22(a, b, dims=NN):
    ahi, alo = split2(a)
    bhi, blo = split2(b)
    return mm(ahi, bhi, dims) + mm(alo, bhi, dims) + mm(ahi, blo, dims)


def sigmoid(x):
    return 1.0 / (1.0 + jnp.exp(-x))


def softplus(x):
    return jnp.maximum(x, 0.0) + jnp.log1p(jnp.exp(-jnp.abs(x)))


def iota(shape, dim):
    return lax.broadcasted_iota(jnp.int32, shape, dim)


def pick(kind, g):
    return (iota((128, GC), 0) == kind * HEADS + HG * g + (iota((128, GC), 1) >> 6)).astype(BF16)


def pick_all(kind):
    return (iota((128, INNER), 0) == kind * HEADS + (iota((128, INNER), 1) >> 6)).astype(BF16)


def cols(g, width=GC):
    return pl.ds(pl.multiple_of(g * width, width), width)


class Exchange:
    def __init__(self, n, rows, chunks, x_ref, y_ref, passes, scratch, start=1, gap=1):
        self.n, self.rows, self.chunks, self.start, self.gap = n, rows, chunks, start, gap
        self.x, self.y, self.passes = x_ref, y_ref, passes
        (self.st, self.rp, self.qr, self.pm, self.pp) = scratch[:5]
        (self.ps, self.pr, self.as_, self.ar, self.bs, self.br) = scratch[5:]
        self.me = lax.axis_index("seq")
        self.partner = self.me + 1 - 2 * (self.me % 2)
        self.has_before = self.me >= 2
        self.has_after = self.me < n - 2

    @staticmethod
    def scratch(rows):
        state = pltpu.VMEM((G, 2, rows, STATE, GC), F32)
        small = pltpu.VMEM((8, INNER), F32)
        dma = pltpu.SemaphoreType.DMA
        return [
            state, state, state, small, small,
            dma((1,)), dma((1,)), dma((G,)), dma((G,)), dma((2, G)), dma((2, G)),
        ]

    def clear(self):
        @pl.when(jnp.logical_not(self.has_before))
        def _():
            self.qr[:, 0] = jnp.zeros_like(self.qr[:, 0])

        @pl.when(jnp.logical_not(self.has_after))
        def _():
            self.qr[:, 1] = jnp.zeros_like(self.qr[:, 1])

    def peers(self, halo):
        found = [(self.partner, True), (self.me - 2, self.has_before), (self.me + 2, self.has_after)]
        if halo:
            other = 2 * self.me - self.partner
            found.append((other, jnp.logical_and(other >= 0, other < self.n)))
        return found

    def greet(self, halo=False):
        for to, there in self.peers(halo):

            @pl.when(there)
            def _(to=to):
                pl.semaphore_signal(
                    pltpu.get_barrier_semaphore(), inc=1, device_id={"seq": to}, device_id_type=MESH)

    def met(self, halo=False):
        count = sum(jnp.asarray(there, jnp.int32) for _, there in self.peers(halo))
        pl.semaphore_wait(pltpu.get_barrier_semaphore(), count)

    def pass_copy(self):
        return pltpu.make_async_remote_copy(
            self.pm, self.pp, self.ps.at[0], self.pr.at[0],
            device_id={"seq": self.partner}, device_id_type=MESH)

    def pair_copy(self, g):
        return pltpu.make_async_remote_copy(
            self.st.at[g], self.rp.at[g], self.as_.at[g], self.ar.at[g],
            device_id={"seq": self.partner}, device_id_type=MESH)

    def chain_copy(self, d, g):
        return pltpu.make_async_remote_copy(
            self.st.at[g, d], self.qr.at[g, d], self.bs.at[d, g], self.br.at[d, g],
            device_id={"seq": self.me + 2 if d == 0 else self.me - 2}, device_id_type=MESH)

    def order(self, d):
        return range(self.chunks) if d == 0 else range(self.chunks - 1, -1, -1)

    def passing(self, d, b, where):
        row = 8 * self.passes[d] + b
        return self.p_ref[row : row + 1, where]

    def set_passes(self, p_ref):
        self.p_ref = p_ref

    def totals_of_passes(self):
        self.pm[...] = jnp.zeros_like(self.pm)
        for d in range(2):
            for r in range(self.rows):
                total = None
                for c in self.order(d):
                    one = self.passing(d, r * self.chunks + c, slice(None))
                    total = one if total is None else total * one
                self.pm[d * self.rows + r : d * self.rows + r + 1, :] = total

    def totals(self, g):
        for d in range(2):
            for r in range(self.rows):
                total = None
                for c in self.order(d):
                    b = r * self.chunks + c
                    one = self.x[b, d, :, cols(g)]
                    total = one if total is None else self.passing(d, b, cols(g)) * total + one
                self.st[g, d, r] = total

    def chain(self, d, g):
        has_in, has_out = (
            (self.has_before, self.has_after) if d == 0 else (self.has_after, self.has_before))
        copy = self.chain_copy(d, g)
        pl.when(has_in)(copy.wait_recv)
        first = self.me % 2 == d
        for r in range(self.rows):
            row = d * self.rows + r
            mine, theirs = self.st[g, d, r], self.rp[g, d, r]
            p_mine = self.pm[row : row + 1, cols(g)]
            p_theirs = self.pp[row : row + 1, cols(g)]
            before = self.qr[g, d, r]
            middle = jnp.where(first, p_mine, p_theirs) * before + jnp.where(first, mine, theirs)
            self.st[g, d, r] = (
                jnp.where(first, p_theirs, p_mine) * middle + jnp.where(first, theirs, mine))
            state = jnp.where(first, before, middle)
            order = list(self.order(d))
            for i, c in enumerate(order):
                b = r * self.chunks + c
                here = state
                if i < len(order) - 1:
                    state = (
                        self.passing(d, b, cols(g)) * state + self.x[b, d, :, cols(g)])
                self.y[b, d, :, cols(g)] = here
        pl.when(has_out)(copy.start)

    def advance(self, step):
        late = self.n // 2 - 1
        place = self.me // 2

        def due(delay, run):
            q = step - self.start - delay
            g = lax.div(jnp.maximum(q, 0), self.gap)
            pl.when(jnp.logical_and(q == g * self.gap, g < G))(lambda: run(g))

        due(0, lambda g: self.pair_copy(g).wait())

        @pl.when(step == self.start)
        def _():
            self.pass_copy().wait_recv()

        due(place, lambda g: self.chain(0, g))
        due(late - place, lambda g: self.chain(1, g))

    def steps(self):
        return self.start + self.gap * (G - 1) + self.n // 2

    def finish(self):
        self.pass_copy().wait_send()

        @pl.loop(0, G)
        def _(g):
            pl.when(self.has_after)(self.chain_copy(0, g).wait_send)
            pl.when(self.has_before)(self.chain_copy(1, g).wait_send)


PIECE = 256


class Reduce:
    STAGES = 8
    SPACE = 2
    LAG = 5

    def __init__(self, far, near_count, half, near, out, scratch):
        self.far, self.near_count, self.half, self.near, self.out = far, near_count, half, near, out
        (self.own, self.r0, self.r1, self.r2, self.r3, self.send, self.recv, self.local) = scratch
        rows, seq = lax.axis_index("rows"), lax.axis_index("seq")
        self.y, self.core, self.z, self.x = rows // 2, rows % 2, seq // 2, seq % 2

    @staticmethod
    def scratch(far):
        def slot(*shape):
            return pltpu.VMEM(shape + (D,), F32)

        dma = pltpu.SemaphoreType.DMA
        return [
            slot(2, 128), slot(far, 128), slot(far, 64), slot(far, 32), slot(far, 24),
            dma((12, far)), dma((12, far)), dma((2, far)),
        ]

    def device(self, x, y, z, core):
        return {"rows": y * 2 + core, "seq": z * 2 + x}

    def greet(self):
        barrier = pltpu.get_barrier_semaphore()
        x, y, z, core = self.x, self.y, self.z, self.core
        peers = [(x, y, z, 1 - core), (1 - x, y, z, core), (x, 1 - y, z, core)] + [
            (x, y, lax.rem(z + d, 4), core) for d in (1, 2, 3)]
        for peer in peers:
            pl.semaphore_signal(barrier, inc=1, device_id=self.device(*peer), device_id_type=MESH)

        @pl.when(self.has_next())
        def _():
            pl.semaphore_signal(
                barrier, inc=1, device_id=self.device(1 - x, y, z + 2 * x - 1, core),
                device_id_type=MESH)

    def has_next(self):
        return jnp.where(self.x == 0, self.z > 0, self.z < 3)

    def met(self):
        pl.semaphore_wait(pltpu.get_barrier_semaphore(), 6 + self.has_next().astype(jnp.int32))

    def turn(self, p):
        return jnp.where(p >= self.far, lax.rem(p, 2), lax.rem(p, 4)) == 1

    def slot(self, p):
        return jnp.where(p < self.far, p, p - self.far)

    def places(self, p):
        x_first = self.turn(p)
        a, b = jnp.where(x_first, self.x, self.y), jnp.where(x_first, self.y, self.x)
        return a * 64, a * 64 + b * 32, a * 64 + b * 32 + self.z * 8

    def copies(self, s, p):
        x, y, z, core = self.x, self.y, self.z, self.core
        i = self.slot(p)
        one, two, three = self.places(p)
        flip_x, flip_y, flip_core = (1 - x, y, z, core), (x, 1 - y, z, core), (x, y, z, 1 - core)

        def mine(start, size):
            return self.r0.at[i, pl.ds(pl.multiple_of(start, 8), size)]

        def final(start, size):
            return self.out.at[pl.ds(pl.multiple_of(p * PIECE + core * 128 + start, 8), size)]

        def copy(src, dst, kind, to):
            return pltpu.make_async_remote_copy(
                src, dst, self.send.at[kind, i], self.recv.at[kind, i],
                device_id=self.device(*to), device_id_type=MESH)

        def over_z(src, dst, kind):
            peers = [(lax.rem(z + d, 4), d - 1) for d in (1, 2, 3)]
            return [copy(src(zz), dst(d), kind + d, (x, y, zz, core)) for zz, d in peers]

        x_first = self.turn(p)
        first = tuple(jnp.where(x_first, u, v) for u, v in zip(flip_x, flip_y))
        second = tuple(jnp.where(x_first, u, v) for u, v in zip(flip_y, flip_x))
        if s == 1:
            return [copy(mine(64 - one, 64), self.r1.at[i], 1, first)]
        if s == 2:
            return [copy(mine(one + 32 - (two - one), 32), self.r2.at[i], 2, second)]
        if s == 3:
            return over_z(
                lambda zz: mine(two + zz * 8, 8), lambda d: self.r3.at[i, pl.ds(8 * d, 8)], 3)
        if s == 4:
            return over_z(lambda zz: mine(three, 8), lambda d: final(three, 8), 6)
        if s == 5:
            return [copy(final(two, 32), final(two, 32), 9, second)]
        if s == 6:
            return [copy(final(one, 64), final(one, 64), 10, first)]
        return [copy(final(0, 128), final(0, 128), 11, flip_core)]

    def near_half(self, p, c):
        return self.near.at[p - self.far, pl.ds(pl.multiple_of(c * 128, 128), 128)]

    def core_copy(self, p, near):
        i = self.slot(p)
        half = (self.near_half if near else self.half)(p, 1 - self.core)
        return pltpu.make_async_remote_copy(
            half, self.r0.at[i], self.send.at[0, i], self.recv.at[0, i],
            device_id=self.device(self.x, self.y, self.z, 1 - self.core), device_id_type=MESH)

    def own_in(self, p):
        return pltpu.make_async_copy(
            self.half(p, self.core), self.own.at[lax.rem(p, 2)], self.local.at[0, self.slot(p)])

    def own_out(self, p):
        i, start = self.slot(p), pl.multiple_of(self.places(p)[2], 8)
        to = p * PIECE + self.core * 128 + start
        return pltpu.make_async_copy(
            self.r0.at[i, pl.ds(start, 8)], self.out.at[pl.ds(pl.multiple_of(to, 8), 8)],
            self.local.at[1, i])

    def begin(self, p):
        @pl.when(p < self.far)
        def _():
            self.own_in(p).start()
            self.core_copy(p, False).start()

        @pl.when(p >= self.far)
        def _():
            self.core_copy(p, True).start()

    def add_core(self, p):
        i = self.slot(p)

        @pl.when(p < self.far)
        def _():
            self.core_copy(p, False).wait()
            self.own_in(p).wait()
            self.r0[i] += self.own[lax.rem(p, 2)]

        @pl.when(p >= self.far)
        def _():
            self.core_copy(p, True).wait()
            self.r0[i] += self.near_half(p, self.core)[...]

    def stage(self, s, p):
        i = self.slot(p)
        starts = self.places(p)
        if s == 1:
            self.add_core(p)
        else:
            for copy in self.copies(s - 1, p):
                copy.wait_recv()

        def kept(which, size):
            return pl.ds(pl.multiple_of(starts[which], 8), size)

        if s == 2:
            self.r0[i, kept(0, 64)] += self.r1[i]
        elif s == 3:
            self.r0[i, kept(1, 32)] += self.r2[i]
        elif s == 4:
            self.r0[i, kept(2, 8)] += self.r3[i, 0:8] + self.r3[i, 8:16] + self.r3[i, 16:24]
            self.own_out(p).start()
        elif s == 5:
            self.own_out(p).wait()
            for done in (1, 2, 3, 4):
                for copy in self.copies(done, p):
                    copy.wait_send()
        if s < self.STAGES:
            for copy in self.copies(s, p):
                copy.start()
        else:
            for done in (5, 6, 7):
                for copy in self.copies(done, p):
                    copy.wait_send()

    def ticks(self):
        return self.far + self.near_count + self.LAG + self.SPACE * self.STAGES

    def tick(self, t):
        for s in range(self.STAGES, -1, -1):
            q = t - self.SPACE * s
            p = jnp.where(q < self.far, q, q - self.LAG)
            due = jnp.logical_and(q >= 0, p < self.far + self.near_count)
            due = jnp.logical_and(due, jnp.logical_or(q < self.far, p >= self.far))

            @pl.when(due)
            def _(s=s, p=p):
                if s == 0:
                    self.begin(p)
                else:
                    self.stage(s, p)


def pieces(x):
    return [x[:, i * STATE : (i + 1) * STATE] for i in range(4)]


START, GAP = 3, 2


def front_kernel(
    n, rows, length, docs,
    tok, ngain, w, weight, cw, cb_i, dtb_i, rate_i, skip_i, starts,
    rounded_o, c_o, p_o, xact_o, y_o, rows_o, q_o, q2_o, pexp_o, sin_o, wide_o, tall_o,
    rext, vhi, vlo, gc, sloc, wst, hsend, hrecv, loads, hs, hr, *scratch,
):
    k = pl.program_id(0)
    chunks = length // C
    blocks = rows * chunks
    ex = Exchange(n, rows, chunks, sloc, sin_o, (0, 1), scratch, START, GAP)
    ex.set_passes(pexp_o)

    def convolved(r, g):
        p = mm(rext[r], w[...], NT)
        p_o[r] = p
        first = PAD - (KW - 1)
        out = wide_o[0:1, cols(g)]
        for i in range(KW):
            out = out + cw[i : i + 1, :] * p[first + i : first + i + length]
        c_o[r * length : (r + 1) * length, :] = out
        return out * sigmoid(out)

    def normed(source):
        scale = lax.rsqrt(jnp.mean(source * source, axis=-1, keepdims=True) + EPS)
        return (source * scale * ngain[...][None, :]).astype(BF16)

    def label_at(r, position):
        found = jnp.int32(0)
        for d in range(docs):
            found += (starts[r, d] <= position).astype(jnp.int32)
        return found.astype(F32)

    def load_steps():
        return pltpu.make_async_copy(
            weight.at[pl.ds(2 * INNER + 4 * STATE, 2 * HEADS)], wst, loads.at[0])

    def halo_copy():
        return pltpu.make_async_remote_copy(
            hsend, hrecv, hs.at[0], hr.at[0],
            device_id={"seq": ex.me + 1}, device_id_type=MESH)

    def tall(ref, count):
        line = jnp.concatenate([ref[...], jnp.zeros((128 - count,), F32)])[None, :]
        return jnp.broadcast_to(line, (8, 128))

    @pl.when(k == 0)
    def _():
        load_steps().start()

        @pl.when(ex.me == 0)
        def _():
            hrecv[...] = jnp.zeros_like(hrecv)

        ex.clear()
        ex.greet(True)
        for r in range(rows):
            hsend[r] = tok[(r + 1) * length - 16 : (r + 1) * length, :].astype(F32)[8:]
        ex.met(True)
        pl.when(ex.me < n - 1)(halo_copy().start)
        for r in range(rows):
            here = slice(r * length, (r + 1) * length)
            out = normed(tok[here, :].astype(F32))
            rext[r, PAD:, :] = out
            rounded_o[here, :] = out
        dtb, rate = tall(dtb_i, 2 * HEADS).T[:48, 0:1], tall(rate_i, 2 * HEADS).T[:48, 0:1]
        lane = iota((48, 128), 1)
        tall_o[...] = jnp.where(lane == 0, dtb, jnp.where(lane == 1, rate, 0.0))
        pick_f, pick_r = pick_all(0), pick_all(2)
        wide_o[0:8, 0:CONV] = jnp.broadcast_to(cb_i[...][None, :], (8, CONV))
        wide_o[8:16, 0:INNER] = mm3(tall(skip_i, HEADS), pick_f)
        upto = (iota((C, C), 0) <= iota((C, C), 1)).astype(BF16)
        load_steps().wait()
        for b in range(blocks):
            here = slice(b * C, (b + 1) * C)
            r, begin = b // chunks, ex.me * length + (b % chunks) * C
            own = jnp.zeros((1, C), F32)
            for d in range(docs):
                own += (starts[r, d] <= begin + iota((1, C), 1)).astype(F32)
            before, first = label_at(r, begin - 1), label_at(r, begin)
            last, after = label_at(r, begin + C - 1), label_at(r, begin + C)
            m0, m1, m2, m3 = [(own == edge).astype(F32) for edge in (before, last, after, first)]
            raw = mm(wst[...], rounded_o[here, :], NT)
            step = softplus(raw + dtb)
            log = -LOG2E * rate * step
            total = mm3(log, upto)
            size = jnp.log(step) * LOG2E
            lf, rc = total[:HEADS], total[HEADS:] - log[HEADS:]
            end_f, end_r = total[:HEADS, C - 1 : C], total[HEADS:, C - 1 : C]
            sf, sr = lf - size[:HEADS], rc + size[HEADS:]
            e_f = jnp.exp2(lf) * m0
            w_f = jnp.exp2(end_f - lf) * step[:HEADS] * m1
            e_r = jnp.exp2(end_r - rc) * m2
            w_r = jnp.exp2(rc) * step[HEADS:] * m3
            labels = jnp.broadcast_to(own, (8, C))
            none = jnp.zeros((24, C), F32)
            rows_o[b] = jnp.concatenate([step, lf, rc, sf, sr, raw, labels], axis=0)
            q = jnp.concatenate([e_f, w_f, e_r, w_r, labels, none], axis=0).T
            q_o[b] = q
            q2_o[b] = jnp.concatenate([lf, rc, sf, sr, labels, none], axis=0).T
            pexp_o[b : b + 1, :] = mm3(q[C - 8 :], pick_f)[7:8]
            pexp_o[8 + b : 9 + b, :] = mm3(q[:8], pick_r)[0:1]
        ex.totals_of_passes()
        pl.when(ex.me > 0)(halo_copy().wait_recv)
        for r in range(rows):
            rext[r, 0:PAD, :] = normed(jnp.concatenate([jnp.zeros((8, D), F32), hrecv[r]], axis=0))
            xact_o[r * length : (r + 1) * length, :] = convolved(r, G)

    @pl.when(jnp.logical_and(k >= 1, k <= G))
    def _():
        g = k - 1
        picks = [pick(1, g), pick(3, g)]
        for r in range(rows):
            v = convolved(r, g)
            hi, lo = split2(v)
            vhi[g, r * length : (r + 1) * length, :] = hi
            vlo[g, r * length : (r + 1) * length, :] = lo
            for c in range(chunks):
                b = r * chunks + c
                vb = v[c * C : (c + 1) * C]
                x = xact_o[b * C : (b + 1) * C, :].astype(BF16)
                for d in range(2):
                    scale = mm2(q_o[b], picks[d])
                    sloc[b, d, :, cols(g)] = mm(
                        x[:, d * STATE : (d + 1) * STATE], (scale * vb).astype(BF16), TN)
        ex.totals(g)
        pl.when(g == 0)(ex.pass_copy().start)
        ex.pair_copy(g).start()

    pl.when(k > 0)(lambda: ex.advance(k - 1))

    @pl.when(k == G + 1)
    def _():
        t_id, s_id = iota((C, C), 0), iota((C, C), 1)
        for b in range(blocks):
            in_f, in_r, rd_f, rd_r = pieces(xact_o[b * C : (b + 1) * C, :])
            gf, gr = mm22(rd_f, in_f, NT), mm22(rd_r, in_r, NT)
            same = jnp.logical_and(q2_o[b][:, 96:97] == rows_o[b, 192:193], t_id != s_id)
            gc[b] = jnp.where(same, jnp.where(t_id > s_id, gf, gr), 0.0)

    @pl.when(jnp.logical_and(k > G, k <= 2 * G))
    def _():
        g = k - 1 - G
        later = iota((C, C), 0) > iota((C, C), 1)
        low = iota((C, 128), 1) < HEAD
        skip = wide_o[8:9, cols(g)]
        for b in range(blocks):
            here = slice(b * C, (b + 1) * C)
            q2 = pltpu.roll(q2_o[b], 128 - HG * g, 1)
            for pair in range(HG // 2):
                at = slice(pair * 128, (pair + 1) * 128)
                v2 = jnp.concatenate([vhi[g, here, at], vlo[g, here, at]], axis=1)
                outs = []
                for h in (2 * pair, 2 * pair + 1):
                    lt, rt = q2[:, h : h + 1], q2[:, HEADS + h : HEADS + h + 1]
                    ls = rows_o[b, pl.ds(96 + HG * g + h, 1), :]
                    rs = rows_o[b, pl.ds(96 + HEADS + HG * g + h, 1), :]
                    x = jnp.exp2(jnp.where(later, lt - ls, rs - rt))
                    o = mm((gc[b] * x).astype(BF16), v2)
                    outs.append(o[:, :128] + o[:, 128:])
                v = vhi[g, here, at].astype(F32) + vlo[g, here, at].astype(F32)
                y_o[here, at] = jnp.where(low, outs[0], outs[1]) + skip[:, at] * v

    @pl.when(k == pl.num_programs(0) - 1)
    def _():
        ex.finish()
        pl.when(ex.me < n - 1)(halo_copy().wait_send)


def middle_kernel(
    y, rounded, tok, cot, q, xact, sin, wg, wo, ogain,
    mixed_o, dy_o, drounded_o, ds_o, dread_o, dq_o, ogain_grad, w_grad,
):
    k = pl.program_id(0)
    x = xact[...].astype(BF16)
    rd_f, rd_r = x[:, 2 * STATE : 3 * STATE], x[:, 3 * STATE :]
    s_f, s_r = sin[0, 0].astype(BF16), sin[0, 1].astype(BF16)
    pick_f, pick_r = pick_all(0), pick_all(2)
    e_f, e_r = mm2(q[0], pick_f), mm2(q[0], pick_r)
    r_f, r_r = mm(rd_f, s_f), mm(rd_r, s_r)
    yv = y[...] + e_f * r_f + e_r * r_r
    gate = mm(rounded[...], wg[...], NT)
    sg = sigmoid(gate)
    silu = gate * sg
    gated = yv * silu
    scale = lax.rsqrt(jnp.mean(gated * gated, axis=-1, keepdims=True) + EPS)
    normed = gated * scale
    out = (normed * ogain[...][None, :]).astype(BF16)
    mixed_o[...] = (tok[...].astype(F32) + mm(out, wo[...])).astype(BF16)
    dout = mm(cot[...], wo[...], NT)
    go = jnp.sum(dout * normed, axis=0, keepdims=True)
    dn = dout * ogain[...][None, :]
    dgated = scale * (dn - normed * jnp.mean(dn * normed, axis=-1, keepdims=True))
    dy = dgated * silu
    dy_o[...] = dy
    dgate = (dgated * yv * sg * (1.0 + gate * (1.0 - sg))).astype(BF16)
    drounded_o[...] = mm(dgate, wg[...])
    u_f, u_r = e_f * dy, e_r * dy
    dq_o[0] = mm2(u_f * r_f, pick_f, NT) + mm2(u_r * r_r, pick_r, NT)
    u_f, u_r = u_f.astype(BF16), u_r.astype(BF16)
    ds_o[0, 1] = mm(rd_f, u_f, TN)
    ds_o[0, 0] = mm(rd_r, u_r, TN)
    dread_o[...] = jnp.concatenate([mm(u_f, s_f, NT), mm(u_r, s_r, NT)], axis=1)

    @pl.when(k == 0)
    def _():
        w_grad[:INNER] = mm(dgate, rounded[...], TN)
        w_grad[INNER:] = mm(out, cot[...], TN)
        ogain_grad[...] = jnp.broadcast_to(go, ogain_grad.shape)

    @pl.when(k > 0)
    def _():
        w_grad[:INNER] += mm(dgate, rounded[...], TN)
        w_grad[INNER:] += mm(out, cot[...], TN)
        ogain_grad[...] += go


def steps_backward(dq, col, row, pg_f, pg_r, raw, step, rate):
    from_t = (iota((C, C), 0) >= iota((C, C), 1)).astype(BF16)
    after_t = (iota((C, C), 0) > iota((C, C), 1)).astype(BF16)
    e_f, w_f, e_r, w_r = [dq[i * HEADS : (i + 1) * HEADS] for i in range(4)]
    cs_f, cs_r = col[:HEADS], col[HEADS : 2 * HEADS]
    d_lf = row[:HEADS] - cs_f + e_f - w_f
    d_rc = cs_r - row[HEADS:] - e_r + w_r
    d_size = jnp.concatenate([cs_f + w_f, cs_r + w_r], axis=0)
    end_f = jnp.sum(w_f, axis=1, keepdims=True) + pg_f
    end_r = jnp.sum(e_r, axis=1, keepdims=True) + pg_r
    d_log = jnp.concatenate([mm3(d_lf, from_t) + end_f, mm3(d_rc, after_t) + end_r], axis=0)
    sg = sigmoid(raw)
    ratio = jnp.where(raw < -15.0, 1.0, sg / jnp.maximum(step, 1e-30))
    d_raw = -rate * d_log * sg + d_size * ratio
    bias = jnp.sum(d_raw, axis=1, keepdims=True)
    rates = -jnp.sum(step * d_log, axis=1, keepdims=True)
    at = iota((2 * HEADS, 128), 1)
    return d_raw, jnp.where(at == 0, bias, jnp.where(at == 1, rates, 0.0))


def back_kernel(
    n, rows, length, far, shared,
    c_i, dy_i, p_i, cw, w, sin,
    xact, rows_i, q_i, q2_i, pexp, dread, dq_i, wide, tall,
    rounded, tok, cot, ngain, ogain_grad,
    ds_i, drounded, w_grad, weight,
    tg_o, total_o, *scratch,
):
    (gct, dgt, dvs, dss, dts, dqs, dins, pgs, z, acc, draw, wst, near, hsend, hrecv, loads, hs, hr) = (
        scratch[:18])
    k = pl.program_id(0)
    chunks = length // C
    blocks = rows * chunks
    near_count = G + 2
    st = near if shared else total_o
    ex = Exchange(n, rows, chunks, z, z, (1, 0), scratch[18:29])
    ex.set_passes(pexp)
    later = iota((C, C), 1) > iota((C, C), 0)
    if shared:

        def half(p, c):
            return w_grad.at[pl.ds(pl.multiple_of(p * PIECE + c * 128, 128), 128)]

        red = Reduce(2 * INNER // PIECE, near_count, half, near, total_o, scratch[29:])

    def load_states():
        return pltpu.make_async_copy(ds_i, z, loads.at[0])

    def load_sum():
        return pltpu.make_async_copy(drounded, acc, loads.at[1])

    def load_steps():
        return pltpu.make_async_copy(
            weight.at[pl.ds(2 * INNER + 4 * STATE, 2 * HEADS)], wst, loads.at[2])

    def halo_copy(g):
        return pltpu.make_async_remote_copy(
            hsend.at[g], hrecv.at[g], hs.at[g], hr.at[g],
            device_id={"seq": ex.me - 1}, device_id_type=MESH)

    @pl.when(k == 0)
    def _():
        load_states().start()
        load_sum().start()
        load_steps().start()

        @pl.when(ex.me == n - 1)
        def _():
            hrecv[...] = jnp.zeros_like(hrecv)

        ex.clear()
        if shared:
            red.greet()
        else:
            ex.greet(True)
        ex.totals_of_passes()
        load_states().wait()

        @pl.loop(0, G)
        def _(g):
            ex.totals(g)

        if shared:
            red.met()
        else:
            ex.met(True)
        ex.pass_copy().start()

        @pl.loop(0, G)
        def _(g):
            ex.pair_copy(g).start()

        if shared:
            red.tick(0)
        differ = iota((C, C), 0) != iota((C, C), 1)
        for b in range(blocks):
            in_f, in_r, rd_f, rd_r = pieces(xact[b * C : (b + 1) * C, :])
            gf, gr = mm22(in_f, rd_f, NT), mm22(in_r, rd_r, NT)
            same = jnp.logical_and(q2_i[b][:, 96:97] == rows_i[b, 192:193], differ)
            gct[b] = jnp.where(same, jnp.where(later, gf, gr), 0.0)
        dgt[...] = jnp.zeros_like(dgt)
        dss[...] = jnp.zeros_like(dss)
        dins[...] = jnp.zeros_like(dins)
        pgs[...] = jnp.zeros_like(pgs)
        dqs[...] = dq_i[...]
        st[G + 1] = jnp.zeros((PIECE, D), F32)
        load_sum().wait()
        load_steps().wait()

    if shared:

        @pl.when(jnp.logical_and(k > 0, k <= far + 1))
        def _():
            red.tick(2 * k)

    @pl.when(k < G)
    def _():
        g = k
        low = iota((C, 128), 1) < HEAD
        lane = iota((C, 128), 1)
        ones = jnp.ones((8, C), BF16)
        skips = jnp.zeros((1, GC), F32)
        skip = wide[8:9, cols(g)]
        for b in range(blocks):
            here = slice(b * C, (b + 1) * C)
            q2 = pltpu.roll(q2_i[b], 128 - HG * g, 1)
            cv = c_i[here, :]
            v = cv * sigmoid(cv)
            dy = dy_i[here, :]
            skips += jnp.sum(dy * v, axis=0, keepdims=True)
            dyhi, dylo = split2(dy)
            vb = v.astype(BF16)
            for pair in range(HG // 2):
                at = slice(pair * 128, (pair + 1) * 128)
                dy2 = jnp.concatenate([dyhi[:, at], dylo[:, at]], axis=1)
                outs = []
                for i in range(2):
                    h = 2 * pair + i
                    mine = low if i == 0 else jnp.logical_not(low)
                    dyh = jnp.where(mine, dyhi[:, at], jnp.zeros((), BF16))
                    dw = mm(vb[:, at], dyh, NT)
                    lt = rows_i[b, pl.ds(48 + HG * g + h, 1), :]
                    rt = rows_i[b, pl.ds(48 + HEADS + HG * g + h, 1), :]
                    ls, rs = q2[:, 48 + h : 49 + h], q2[:, 72 + h : 73 + h]
                    x = jnp.exp2(jnp.where(later, lt - ls, rs - rt))
                    dwx = dw * x
                    dgt[b] += dwx
                    gb = gct[b]
                    o = mm((gb * x).astype(BF16), dy2)
                    outs.append(o[:, :128] + o[:, 128:])
                    de = dwx * gb
                    de_f = jnp.where(later, de, 0.0).astype(BF16)
                    de_r = jnp.where(later, 0.0, de).astype(BF16)
                    hot_f = (lane == HG * g + h).astype(BF16)
                    hot_r = (lane == HEADS + HG * g + h).astype(BF16)
                    dss[b] += mm(de_f, hot_f) + mm(de_r, hot_r)
                    dts[b, pl.ds(HG * g + h, 1), :] = mm(ones, de_f)[0:1]
                    dts[b, pl.ds(HEADS + HG * g + h, 1), :] = mm(ones, de_r)[0:1]
                dvs[g, here, at] = jnp.where(low, outs[0], outs[1]) + skip[:, at] * dy[:, at]
        line = pl.multiple_of(120 + 8 * (g // 3), 8)
        st[G + 1, pl.ds(line, 8), cols(lax.rem(g, 3))] = jnp.broadcast_to(skips, (8, GC))

    ex.advance(k)

    def send_halo(g):
        for r in range(rows):
            hsend[g, r] = dvs[g, r * length : r * length + 8, :]
        pl.when(ex.me > 0)(halo_copy(g).start)

    @pl.when(jnp.logical_and(k >= far, k < far + G))
    def _():
        g = k - far
        picks = [pick(1, g), pick(3, g)]
        for b in range(blocks):
            here = slice(b * C, (b + 1) * C)
            cv = c_i[here, :]
            sg = sigmoid(cv)
            v = cv * sg
            x = xact[here, :].astype(BF16)
            dv = dvs[g, here, :]
            for d in range(2):
                zf = z[b, 1 - d, :, cols(g)]
                zb = zf.astype(BF16)
                weight = mm2(q_i[b], picks[d])
                m = mm(x[:, d * STATE : (d + 1) * STATE], zb)
                dv += weight * m
                u = weight * v
                dqs[b] += mm2(u * m, picks[d], NT)
                at = slice(d * STATE, (d + 1) * STATE)
                dins[b, :, at] += mm(u.astype(BF16), zb, NT)
                pgs[8 * d + b : 8 * d + b + 1, cols(g)] = pexp[
                    8 * d + b : 8 * d + b + 1, cols(g)
                ] * jnp.sum(zf * sin[b, d], axis=0, keepdims=True)
            dvs[g, here, :] = dv * (sg * (1.0 + cv * (1.0 - sg)))
        send_halo(g)

    @pl.when(k == far + G)
    def _():
        differ = iota((C, C), 0) != iota((C, C), 1)
        for b in range(blocks):
            here = slice(b * C, (b + 1) * C)
            same = jnp.logical_and(q2_i[b][:, 96:97] == rows_i[b, 192:193], differ)
            dg = jnp.where(same, dgt[b], 0.0)
            dg_f = jnp.where(later, dg, 0.0).astype(BF16)
            dg_r = jnp.where(later, 0.0, dg).astype(BF16)
            in_f, in_r, rd_f, rd_r = pieces(xact[here, :].astype(BF16))
            dx = jnp.concatenate(
                [
                    dins[b, :, :STATE] + mm(dg_f, rd_f),
                    dins[b, :, STATE:] + mm(dg_r, rd_r),
                    dread[here, :STATE] + mm(dg_f, in_f, TN),
                    dread[here, STATE:] + mm(dg_r, in_r, TN),
                ],
                axis=1,
            )
            cv = c_i[here, :]
            sg = sigmoid(cv)
            dvs[G, here, :] = dx * (sg * (1.0 + cv * (1.0 - sg)))
        send_halo(G)
        pg_f = mm2(pgs[0:8], pick_all(0), NT).T
        pg_r = mm2(pgs[8:16], pick_all(2), NT).T
        sums = jnp.zeros((2 * HEADS, 128), F32)
        for b in range(blocks):
            d_raw, small = steps_backward(
                dqs[b].T, dss[b].T, dts[b], pg_f[:HEADS, b : b + 1],
                pg_r[2 * HEADS : 3 * HEADS, b : b + 1], rows_i[b, 144:192] + tall[:, 0:1],
                rows_i[b, 0:48], tall[:, 1:2])
            draw[:, b * C : (b + 1) * C] = d_raw.astype(BF16)
            sums += small
        st[G + 1, 0:48] = mm(draw[...], rounded[...])
        st[G + 1, 48:96, 0:128] = sums

    if shared:

        @pl.when(jnp.logical_and(k > 0, k <= far))
        def _():
            red.tick(2 * k + 1)

        @pl.when(k == 0)
        def _():
            red.tick(1)

        @pl.when(k == far + 1)
        def _():
            red.tick(2 * k + 1)
            red.tick(2 * k + 2)

    @pl.when(k > far)
    def _():
        g = k - far - 1
        pl.when(ex.me < n - 1)(halo_copy(g).wait_recv)
        parts = []
        taps = [jnp.zeros((1, GC), F32) for _ in range(KW)]
        bias = jnp.zeros((1, GC), F32)
        for r in range(rows):
            own = dvs[g, r * length : (r + 1) * length, :]
            ext = jnp.concatenate([own, hrecv[g, r]], axis=0)
            total = None
            for i in range(KW):
                one = cw[i : i + 1, :] * ext[KW - 1 - i : KW - 1 - i + length]
                total = one if total is None else total + one
                first = PAD - (KW - 1) + i
                taps[i] += jnp.sum(own * p_i[r, first : first + length, :], axis=0, keepdims=True)
            bias += jnp.sum(own, axis=0, keepdims=True)
            parts.append(total.astype(BF16))
        both = jnp.concatenate(parts, axis=0)
        st[g] = mm(both, rounded[...], TN)
        line = pl.multiple_of(136 + 8 * (g // 3), 8)
        st[G + 1, pl.ds(line, 8), cols(lax.rem(g, 3))] = jnp.concatenate(
            taps + [bias, jnp.zeros((3, GC), F32)], axis=0)
        if shared:
            red.tick(red.far + red.LAG + g)
        acc[...] += mm(both, w[...])

    @pl.when(k == far + G + 1)
    def _():
        acc[...] += mm(draw[...], wst[...], TN)
        gains = jnp.zeros((1, D), F32)
        for b in range(blocks):
            here = slice(b * C, (b + 1) * C)
            source = tok[here, :].astype(F32)
            scale = lax.rsqrt(jnp.mean(source * source, axis=-1, keepdims=True) + EPS)
            m = source * scale
            d_rounded = acc[here, :]
            gains += jnp.sum(d_rounded * m, axis=0, keepdims=True)
            nn = d_rounded * ngain[...][None, :]
            d_source = scale * (nn - m * jnp.mean(nn * m, axis=-1, keepdims=True))
            tg_o[here, :] = (cot[here, :].astype(F32) + d_source).astype(BF16)
        st[G + 1, 96:104] = jnp.broadcast_to(gains, (8, D))
        for i in range(2):
            st[G + 1, 104 + 8 * i : 112 + 8 * i] = ogain_grad[:, i * D : (i + 1) * D]
        if shared:

            @pl.loop(red.far + red.LAG + G + 1, red.ticks())
            def _(t):
                red.tick(t)

        ex.finish()

        @pl.loop(0, G + 1)
        def _(g):
            pl.when(ex.me > 0)(halo_copy(g).wait_send)


def finish_kernel(
    total, in_o, out_o, ng_o, cw_o, cb_o, dtb_o, rate_o, skip_o, og_o, held, arrive, leave,
):
    count = total.shape[0] // PIECE
    gates = INNER // PIECE

    def read(i):
        return pltpu.make_async_copy(
            total.at[pl.ds(i * PIECE, PIECE)], held.at[i], arrive.at[i])

    def write(i):
        size = PIECE
        if i < gates:
            to = in_o.at[pl.ds(i * PIECE, PIECE)]
        elif i < 2 * gates:
            to = out_o.at[pl.ds((i - gates) * PIECE, PIECE)]
        else:
            size = PIECE if i < count - 1 else 2 * HEADS
            to = in_o.at[pl.ds((i - gates) * PIECE, size)]
        return pltpu.make_async_copy(held.at[i, pl.ds(0, size)], to, leave.at[i])

    for i in range(count):
        read(i).start()
    for i in range(count):
        read(i).wait()
        write(i).start()
    rest = held.at[count - 1]
    ng_o[...] = rest[96:97, :][0]
    og_o[...] = jnp.concatenate([rest[104:105, :], rest[112:113, :]], axis=1)[0]
    lines = jnp.concatenate([rest[120:128, :], rest[128:136, :]], axis=1)
    skip_o[...] = mm3(lines, pick_all(0), NT)[0, 0:HEADS]
    both = jnp.concatenate([rest[48:96, 0:128], jnp.zeros((80, 128), F32)], axis=0).T
    dtb_o[...] = both[0, 0 : 2 * HEADS]
    rate_o[...] = both[1, 0 : 2 * HEADS]
    taps = jnp.concatenate([rest[136:144, :], rest[144:152, :], rest[152:160, :GC]], axis=1)
    cw_o[...] = taps[:KW]
    cb_o[...] = taps[KW]
    for i in range(count):
        write(i).wait()


def whole(shape):
    zeros = (0,) * len(shape)
    return pl.BlockSpec(shape, lambda k: zeros, pipeline_mode=pl.Buffered(1))


def struct(shape, dtype=F32):
    return jax.ShapeDtypeStruct(shape, dtype)


def on_device(
    tokens, doc_starts, norm_gain, in_weight, conv_weight, conv_bias, dt_bias, decay_rate,
    skip_scale, out_gain, out_weight, cotangent,
):
    n = lax.axis_size("seq")
    rows, length, _ = tokens.shape
    docs = doc_starts.shape[1]
    chunks = length // C
    blocks = rows * chunks
    count = rows * length
    weight = in_weight.T
    tok, cot = tokens.reshape(count, D), cotangent.reshape(count, D)
    anywhere = pl.BlockSpec(memory_space=pl.ANY)

    params = dict(vmem_limit_bytes=VMEM_LIMIT)
    dims = ("arbitrary",)

    def col(k):
        return jnp.where(k == 0, G, jnp.minimum(k - 1, G - 1))

    def ycol(k):
        return jnp.clip(k - 1 - G, 0, G - 1)

    front_steps = max(2 * G, START + GAP * (G - 1) + n // 2) + 1
    rounded, c, p, xact, y, rowsv, q, q2, pexp, sin, wide, tall = pl.pallas_call(
        lambda *refs: front_kernel(n, rows, length, docs, *refs),
        grid=(front_steps,),
        in_specs=[
            whole((count, D)), whole((D,)),
            pl.BlockSpec((GC, D), lambda k: (G + col(k), 0)), anywhere,
            pl.BlockSpec((KW, GC), lambda k: (0, col(k))),
            whole((CONV,)), whole((2 * HEADS,)), whole((2 * HEADS,)), whole((HEADS,)),
            pl.BlockSpec(memory_space=pltpu.SMEM),
        ],
        out_specs=[
            whole((count, D)),
            pl.BlockSpec((count, GC), lambda k: (0, col(k))),
            pl.BlockSpec((rows, PAD + length, GC), lambda k: (0, 0, col(k))),
            whole((count, GC)),
            pl.BlockSpec((count, GC), lambda k: (0, ycol(k))),
            whole((blocks, 200, C)), whole((blocks, C, 128)), whole((blocks, C, 128)),
            whole((16, INNER)), whole((blocks, 2, STATE, INNER)), whole((16, CONV)),
            whole((2 * HEADS, 128)),
        ],
        out_shape=[
            struct((count, D), BF16), struct((count, CONV)), struct((rows, PAD + length, CONV)),
            struct((count, GC)), struct((count, INNER)), struct((blocks, 200, C)),
            struct((blocks, C, 128)), struct((blocks, C, 128)), struct((16, INNER)),
            struct((blocks, 2, STATE, INNER)), struct((16, CONV)), struct((2 * HEADS, 128)),
        ],
        scratch_shapes=[
            pltpu.VMEM((rows, PAD + length, D), BF16),
            pltpu.VMEM((G, count, GC), BF16), pltpu.VMEM((G, count, GC), BF16),
            pltpu.VMEM((blocks, C, C), F32), pltpu.VMEM((blocks, 2, STATE, INNER), F32),
            pltpu.VMEM((2 * HEADS, D), BF16),
            pltpu.VMEM((rows, 8, D), F32), pltpu.VMEM((rows, 8, D), F32),
            pltpu.SemaphoreType.DMA((1,)), pltpu.SemaphoreType.DMA((1,)),
            pltpu.SemaphoreType.DMA((1,)),
            *Exchange.scratch(rows),
        ],
        compiler_params=pltpu.CompilerParams(
            dimension_semantics=dims, collective_id=0, has_side_effects=True, **params),
        name="front",
    )(tok, norm_gain, weight, weight, conv_weight, conv_bias, dt_bias, decay_rate, skip_scale,
      doc_starts)

    def by_block(shape):
        zeros = (0,) * (len(shape) - 1)
        return pl.BlockSpec(shape, lambda k: (k,) + zeros)

    mixed, dy, drounded, ds, dread, dq, ogain_grad, w_grad = pl.pallas_call(
        middle_kernel,
        grid=(blocks,),
        in_specs=[
            by_block((C, INNER)), by_block((C, D)), by_block((C, D)), by_block((C, D)),
            by_block((1, C, 128)), by_block((C, GC)), by_block((1, 2, STATE, INNER)),
            whole((INNER, D)), whole((INNER, D)), whole((INNER,)),
        ],
        out_specs=[
            by_block((C, D)), by_block((C, INNER)), by_block((C, D)),
            by_block((1, 2, STATE, INNER)), by_block((C, 128)), by_block((1, C, 128)),
            whole((8, INNER)), whole((2 * INNER, D)),
        ],
        out_shape=[
            struct((count, D), BF16), struct((count, INNER)), struct((count, D)),
            struct((blocks, 2, STATE, INNER)), struct((count, 128)), struct((blocks, C, 128)),
            struct((8, INNER)), struct((2 * INNER, D)),
        ],
        compiler_params=pltpu.CompilerParams(dimension_semantics=dims, **params),
        name="middle",
    )(y, rounded, tok, cot, q, xact, sin, weight, out_weight, out_gain)

    far = max(G, n // 2 + 1)
    shared = n == 8 and lax.axis_size("rows") == 4

    def vcol(k):
        return jnp.where(k < far, jnp.minimum(k, G - 1), jnp.minimum(k - far, G))

    def first_pass(k):
        return jnp.minimum(k, G - 1)

    def second_pass(k):
        return jnp.clip(k - far, 0, G - 1)

    def conv_pass(k):
        return jnp.clip(k - far - 1, 0, G)

    far_pieces = 2 * INNER // PIECE
    total_rows = (far_pieces + G + 2) * PIECE
    tg, total = pl.pallas_call(
        lambda *refs: back_kernel(n, rows, length, far, shared, *refs),
        grid=(far + G + 2,),
        in_specs=[
            pl.BlockSpec((count, GC), lambda k: (0, vcol(k))),
            pl.BlockSpec((count, GC), lambda k: (0, first_pass(k))),
            pl.BlockSpec((rows, PAD + length, GC), lambda k: (0, 0, conv_pass(k))),
            pl.BlockSpec((KW, GC), lambda k: (0, conv_pass(k))),
            pl.BlockSpec((GC, D), lambda k: (G + conv_pass(k), 0)),
            pl.BlockSpec((blocks, 2, STATE, GC), lambda k: (0, 0, 0, second_pass(k))),
            whole((count, GC)), whole((blocks, 200, C)), whole((blocks, C, 128)),
            whole((blocks, C, 128)), whole((16, INNER)), whole((count, 128)),
            whole((blocks, C, 128)), whole((16, CONV)), whole((2 * HEADS, 128)),
            whole((count, D)), whole((count, D)), whole((count, D)), whole((D,)),
            whole((8, INNER)), anywhere, anywhere, anywhere, anywhere,
        ],
        out_specs=[whole((count, D)), anywhere if shared else whole((G + 2, PIECE, D))],
        out_shape=[
            struct((count, D), BF16),
            struct((total_rows, D) if shared else (G + 2, PIECE, D)),
        ],
        scratch_shapes=[
            pltpu.VMEM((blocks, C, C), F32), pltpu.VMEM((blocks, C, C), F32),
            pltpu.VMEM((G + 1, count, GC), F32), pltpu.VMEM((blocks, C, 128), F32),
            pltpu.VMEM((blocks, 2 * HEADS, C), F32), pltpu.VMEM((blocks, C, 128), F32),
            pltpu.VMEM((blocks, C, 128), F32), pltpu.VMEM((16, INNER), F32),
            pltpu.VMEM((blocks, 2, STATE, INNER), F32), pltpu.VMEM((count, D), F32),
            pltpu.VMEM((2 * HEADS, count), BF16), pltpu.VMEM((2 * HEADS, D), BF16),
            pltpu.VMEM((G + 2, PIECE, D) if shared else (8, 128), F32),
            pltpu.VMEM((G + 1, rows, 8, GC), F32), pltpu.VMEM((G + 1, rows, 8, GC), F32),
            pltpu.SemaphoreType.DMA((3,)), pltpu.SemaphoreType.DMA((G + 1,)),
            pltpu.SemaphoreType.DMA((G + 1,)),
            *Exchange.scratch(rows), *(Reduce.scratch(far_pieces) if shared else []),
        ],
        compiler_params=pltpu.CompilerParams(
            dimension_semantics=dims, collective_id=1, has_side_effects=True,
            vmem_limit_bytes=63 * 1024 * 1024),
        name="back",
    )(c, dy, p, conv_weight, weight, sin, xact, rowsv, q, q2, pexp, dread, dq, wide, tall,
      rounded, tok, cot, norm_gain, ogain_grad, ds, drounded, w_grad, weight)

    if not shared:
        total = lax.psum(jnp.concatenate([w_grad, total.reshape(-1, D)], axis=0), ("rows", "seq"))
    held = total_rows // PIECE
    inside = pl.BlockSpec(memory_space=pltpu.VMEM)
    in_grad, out_grad, ng, cw, cb, dtb, rate, skip, og = pl.pallas_call(
        finish_kernel,
        in_specs=[anywhere],
        out_specs=[anywhere, anywhere] + [inside] * 7,
        out_shape=[
            struct((2 * INNER + 4 * STATE + 2 * HEADS, D)), struct((INNER, D)), struct((D,)),
            struct((KW, CONV)), struct((CONV,)), struct((2 * HEADS,)), struct((2 * HEADS,)),
            struct((HEADS,)), struct((INNER,)),
        ],
        scratch_shapes=[
            pltpu.VMEM((held, PIECE, D), F32), pltpu.SemaphoreType.DMA((held,)),
            pltpu.SemaphoreType.DMA((held,)),
        ],
        compiler_params=pltpu.CompilerParams(**params),
        name="finish",
    )(total)
    return (
        mixed.reshape(tokens.shape), tg.reshape(tokens.shape), ng, in_grad.T, cw, cb, dtb, rate,
        skip, og, out_grad,
    )


def solution(mesh):
    local = P("rows", "seq", None)
    return jax.shard_map(
        on_device,
        mesh=mesh,
        in_specs=(local, P("rows", None)) + (P(),) * 9 + (local,),
        out_specs=(local, local) + (P(),) * 9,
        check_vma=False,
    )
```

time: 554 us -> 344 us (0.62); the launches traced: 545 us -> 342 us
  waiting for transfers between devices: 222 us -> 0 us
  Pallas kernels: 209 us -> 340 us
  blocking collectives: 41.5 us -> 0 us
  local copies, waits for them, and re-layouts: 38.8 us -> 1.15 us
  between operations: 14.7 us -> 0.88 us
  other arithmetic: 12.1 us -> 0 us
  starting transfers between devices: 6.15 us -> 0 us
    psum x1 -> x0, waiting for transfers between devices: 217 us -> none  [on_device(): lax.psum((ng_grad[0], in_weight_grad, cw_grad[:KW], cb_grad[0], small[:,...]
    pallas_call x3, Pallas kernels: 169 us -> 299 us  [the longest x1 209 us: on_device(): pl.pallas_call(lambda *refs: back_kernel(n, rows, length, far, shared, *r...]
    psum x1 -> x0, blocking collectives: 41.5 us -> none  [on_device(): lax.psum((ng_grad[0], in_weight_grad, cw_grad[:KW], cb_grad[0], small[:,...]
    unnamed x21 -> x3, local copies, waits for them, and re-layouts: 25 us -> 1.15 us
    concatenate x1 -> x0, other arithmetic: 8.68 us -> none  [on_device(): in_weight_grad = jnp.concatenate([wg_grad, wc_grad, ws_grad.T], axis=1)]
    ppermute x2 -> x0, starting transfers between devices: 6.11 us -> none  [shifted(): lax.ppermute(value, axis, [(i, i + steps) for i in range(leading, last)])]
  transfers between devices with their start and end apart: 3 -> 0, of which waited for: 2 -> 0; matrix products, arithmetic and copies ran while one was open for 4% -> 0% of each run, Pallas kernels for 0% -> 0%
where the time goes in v2:
time: 344 us; the launch traced here: 342 us
  Pallas kernels  340 us (99%)
    pallas_call x1, Pallas kernels, on_device(): pl.pallas_call(lambda *refs: back_kernel(n, rows, length, far, shared, *r...  209 us
    pallas_call x1, Pallas kernels, on_device(): pl.pallas_call(lambda *refs: front_kernel(n, rows, length, docs, *refs),...  78.1 us
    pallas_call x1, Pallas kernels, on_device(): pl.pallas_call(middle_kernel, grid=(blocks,), in_specs=[by_block((C, INNE...  41.3 us
    pallas_call x1, Pallas kernels, on_device(): pl.pallas_call(finish_kernel, in_specs=[anywhere], out_specs=[anywhere, a...  11.8 us

profile of v2, /device:TPU:0, one launch (start us, length us, event | category | flops | bytes accessed | tf_op | source)
XLA Modules:
  0.0 342.3 jit_solution(7091995528236161255)
XLA Ops:
  0.6 78.1 %front.1 = (bf16[1024,768]{1,0:T(8,128)(2,1)}, f32[1024,1792]{1,0:T(8,128)}, f32[2,528,1792]{2,1,0:T(8,128)}, f32[1024,256]{1,0:T(8,128)}, f32[1024,1536]{1,0:T(...) custom-call(bf16[1024,768]{1,0:T(8,128)(2,1)} %bitcast.11, ...), custom_call_target="tpu_custom_call" | custom-call | tf_op jit(solution)/shard_map/front/pallas_call | solution.py:1029
  78.7 41.3 %middle.1 = (bf16[1024,768]{1,0:T(8,128)(2,1)}, f32[1024,1536]{1,0:T(8,128)}, f32[1024,768]{1,0:T(8,128)}, f32[4,2,64,1536]{3,2,1,0:T(8,128)}, f32[1024,128]{1,0...) custom-call(f32[1024,1536]{1,0:T(8,128)} %get-tuple-element.42.y, ...), custom_call_target="tpu_custom_call" | custom-call | tf_op jit(solution)/shard_map/middle/pallas_call | solution.py:1075
  120.0 209.1 %back.1 = (bf16[1024,768]{1,0:T(8,128)(2,1)}, f32[5120,768]{1,0:T(8,128)}) custom-call(f32[1024,1792]{1,0:T(8,128)} %get-tuple-element.48.refs_0_, f32[1024,1536]{1,0:T(8,128)} %get-tuple-element.49.refs_1_, f32[2,528,1792]{2,1,0:T(8,128)} %get-tuple-element.50.refs_2_, f32[4,1792]{1,0:T(4,128)} %refs_3_.1, bf16[3376,768]{1,0:T(8,128)(2,1)} %bitcast.9, ...), custom_call_target="tpu_custom_call" | custom-call | tf_op jit(solution)/shard_map/back/pallas_call | solution.py:1114
  329.1 0.0 copy-start
  329.1 11.8 %finish.1 = (f32[3376,768]{1,0:T(8,128)}, f32[1536,768]{1,0:T(8,128)}, f32[768]{0:T(1024)}, f32[4,1792]{1,0:T(4,128)}, f32[1792]{0:T(1024)}, /*index=5*/f32[48]{...) custom-call(f32[5120,768]{1,0:T(8,128)} %get-tuple-element.63.total), custom_call_target="tpu_custom_call" | custom-call | tf_op jit(solution)/shard_map/finish/pallas_call | solution.py:1159
  341.0 0.0 copy-done
  341.0 1.1 copy.24
Async XLA Ops:
  329.1 11.8 %copy-start = (bf16[1024,768]{1,0:T(8,128)(2,1)S(1)}, bf16[1024,768]{1,0:T(8,128)(2,1)}, u32[]{:S(2)}) copy-start(bf16[1024,768]{1,0:T(8,128)(2,1)} %get-tuple-element.62) | copy-start | bytes 4718596

commit v3 on v2

--- a/solution.py
+++ b/solution.py
@@ -43,13 +43,15 @@
 
 
 def mm2(a, b, dims=NN):
-    hi, lo = split2(a)
-    return mm(hi, b, dims) + mm(lo, b, dims)
+    count = a.shape[0]
+    both = mm(jnp.concatenate(split2(a), axis=0), b, dims)
+    return both[:count] + both[count:]
 
 
 def mm3(a, b, dims=NN):
-    hi, mid, lo = split3(a)
-    return mm(hi, b, dims) + mm(mid, b, dims) + mm(lo, b, dims)
+    count = a.shape[0]
+    every = mm(jnp.concatenate(split3(a), axis=0), b, dims)
+    return every[:count] + every[count : 2 * count] + every[2 * count :]
 
 
 def mm22(a, b, dims=NN):
@@ -281,7 +283,7 @@
         pl.semaphore_wait(pltpu.get_barrier_semaphore(), 6 + self.has_next().astype(jnp.int32))
 
     def turn(self, p):
-        return jnp.where(p >= self.far, lax.rem(p, 2), lax.rem(p, 4)) == 1
+        return lax.rem(p, 2) == 1
 
     def slot(self, p):
         return jnp.where(p < self.far, p, p - self.far)
@@ -429,7 +431,7 @@
     return [x[:, i * STATE : (i + 1) * STATE] for i in range(4)]
 
 
-START, GAP = 3, 2
+START, GAP = 2, 1
 
 
 def front_kernel(
@@ -501,7 +503,7 @@
         tall_o[...] = jnp.where(lane == 0, dtb, jnp.where(lane == 1, rate, 0.0))
         pick_f, pick_r = pick_all(0), pick_all(2)
         wide_o[0:8, 0:CONV] = jnp.broadcast_to(cb_i[...][None, :], (8, CONV))
-        wide_o[8:16, 0:INNER] = mm3(tall(skip_i, HEADS), pick_f)
+        lines = [tall(skip_i, HEADS)]
         upto = (iota((C, C), 0) <= iota((C, C), 1)).astype(BF16)
         load_steps().wait()
         for b in range(blocks):
@@ -531,8 +533,14 @@
             q = jnp.concatenate([e_f, w_f, e_r, w_r, labels, none], axis=0).T
             q_o[b] = q
             q2_o[b] = jnp.concatenate([lf, rc, sf, sr, labels, none], axis=0).T
-            pexp_o[b : b + 1, :] = mm3(q[C - 8 :], pick_f)[7:8]
-            pexp_o[8 + b : 9 + b, :] = mm3(q[:8], pick_r)[0:1]
+            lines += [q[C - 8 :], q[:8]]
+        if len(lines) % 2:
+            lines.append(lines[0])
+        wide_f, wide_r = [mm3(jnp.concatenate(lines, axis=0), pick) for pick in (pick_f, pick_r)]
+        wide_o[8:16, 0:INNER] = wide_f[0:8]
+        for b in range(blocks):
+            pexp_o[b : b + 1, :] = wide_f[16 * b + 15 : 16 * b + 16]
+            pexp_o[8 + b : 9 + b, :] = wide_r[16 * b + 16 : 16 * b + 17]
         ex.totals_of_passes()
         pl.when(ex.me > 0)(halo_copy().wait_recv)
         for r in range(rows):
@@ -603,8 +611,11 @@
 def middle_kernel(
     y, rounded, tok, cot, q, xact, sin, wg, wo, ogain,
     mixed_o, dy_o, drounded_o, ds_o, dread_o, dq_o, ogain_grad, w_grad,
+    outs, dgates,
 ):
     k = pl.program_id(0)
+    here = pl.ds(pl.multiple_of(k * C, C), C)
+    rounded_b, cot_b = rounded[here, :], cot[here, :]
     x = xact[...].astype(BF16)
     rd_f, rd_r = x[:, 2 * STATE : 3 * STATE], x[:, 3 * STATE :]
     s_f, s_r = sin[0, 0].astype(BF16), sin[0, 1].astype(BF16)
@@ -612,21 +623,23 @@
     e_f, e_r = mm2(q[0], pick_f), mm2(q[0], pick_r)
     r_f, r_r = mm(rd_f, s_f), mm(rd_r, s_r)
     yv = y[...] + e_f * r_f + e_r * r_r
-    gate = mm(rounded[...], wg[...], NT)
+    gate = mm(rounded_b, wg[...], NT)
     sg = sigmoid(gate)
     silu = gate * sg
     gated = yv * silu
     scale = lax.rsqrt(jnp.mean(gated * gated, axis=-1, keepdims=True) + EPS)
     normed = gated * scale
     out = (normed * ogain[...][None, :]).astype(BF16)
+    outs[here, :] = out
     mixed_o[...] = (tok[...].astype(F32) + mm(out, wo[...])).astype(BF16)
-    dout = mm(cot[...], wo[...], NT)
+    dout = mm(cot_b, wo[...], NT)
     go = jnp.sum(dout * normed, axis=0, keepdims=True)
     dn = dout * ogain[...][None, :]
     dgated = scale * (dn - normed * jnp.mean(dn * normed, axis=-1, keepdims=True))
     dy = dgated * silu
     dy_o[...] = dy
     dgate = (dgated * yv * sg * (1.0 + gate * (1.0 - sg))).astype(BF16)
+    dgates[here, :] = dgate
     drounded_o[...] = mm(dgate, wg[...])
     u_f, u_r = e_f * dy, e_r * dy
     dq_o[0] = mm2(u_f * r_f, pick_f, NT) + mm2(u_r * r_r, pick_r, NT)
@@ -637,15 +650,18 @@
 
     @pl.when(k == 0)
     def _():
-        w_grad[:INNER] = mm(dgate, rounded[...], TN)
-        w_grad[INNER:] = mm(out, cot[...], TN)
         ogain_grad[...] = jnp.broadcast_to(go, ogain_grad.shape)
 
     @pl.when(k > 0)
     def _():
-        w_grad[:INNER] += mm(dgate, rounded[...], TN)
-        w_grad[INNER:] += mm(out, cot[...], TN)
         ogain_grad[...] += go
+
+    @pl.when(k == pl.num_programs(0) - 1)
+    def _():
+        for i in range(G):
+            at = slice(i * GC, (i + 1) * GC)
+            w_grad[at] = mm(dgates[:, at], rounded[...], TN)
+            w_grad[INNER + i * GC : INNER + (i + 1) * GC] = mm(outs[:, at], cot[...], TN)
 
 
 def steps_backward(dq, col, row, pg_f, pg_r, raw, step, rate):
@@ -740,8 +756,6 @@
         def _(g):
             ex.pair_copy(g).start()
 
-        if shared:
-            red.tick(0)
         differ = iota((C, C), 0) != iota((C, C), 1)
         for b in range(blocks):
             in_f, in_r, rd_f, rd_r = pieces(xact[b * C : (b + 1) * C, :])
@@ -756,12 +770,6 @@
         st[G + 1] = jnp.zeros((PIECE, D), F32)
         load_sum().wait()
         load_steps().wait()
-
-    if shared:
-
-        @pl.when(jnp.logical_and(k > 0, k <= far + 1))
-        def _():
-            red.tick(2 * k)
 
     @pl.when(k < G)
     def _():
@@ -867,8 +875,8 @@
             sg = sigmoid(cv)
             dvs[G, here, :] = dx * (sg * (1.0 + cv * (1.0 - sg)))
         send_halo(G)
-        pg_f = mm2(pgs[0:8], pick_all(0), NT).T
-        pg_r = mm2(pgs[8:16], pick_all(2), NT).T
+        pg_f = mm2(pgs[...], pick_all(0), NT)[0:8].T
+        pg_r = mm2(pgs[...], pick_all(2), NT)[8:16].T
         sums = jnp.zeros((2 * HEADS, 128), F32)
         for b in range(blocks):
             d_raw, small = steps_backward(
@@ -880,20 +888,14 @@
         st[G + 1, 0:48] = mm(draw[...], rounded[...])
         st[G + 1, 48:96, 0:128] = sums
 
+    def until(k):
+        return jnp.maximum(2 * (k - 2), 0)
+
     if shared:
 
-        @pl.when(jnp.logical_and(k > 0, k <= far))
-        def _():
-            red.tick(2 * k + 1)
-
-        @pl.when(k == 0)
-        def _():
-            red.tick(1)
-
-        @pl.when(k == far + 1)
-        def _():
-            red.tick(2 * k + 1)
-            red.tick(2 * k + 2)
+        @pl.loop(jnp.where(k == 0, 0, until(k - 1)), until(k))
+        def _(t):
+            red.tick(t)
 
     @pl.when(k > far)
     def _():
@@ -918,8 +920,6 @@
         line = pl.multiple_of(136 + 8 * (g // 3), 8)
         st[G + 1, pl.ds(line, 8), cols(lax.rem(g, 3))] = jnp.concatenate(
             taps + [bias, jnp.zeros((3, GC), F32)], axis=0)
-        if shared:
-            red.tick(red.far + red.LAG + g)
         acc[...] += mm(both, w[...])
 
     @pl.when(k == far + G + 1)
@@ -941,7 +941,7 @@
             st[G + 1, 104 + 8 * i : 112 + 8 * i] = ogain_grad[:, i * D : (i + 1) * D]
         if shared:
 
-            @pl.loop(red.far + red.LAG + G + 1, red.ticks())
+            @pl.loop(until(k), red.ticks())
             def _(t):
                 red.tick(t)
 
@@ -982,7 +982,7 @@
     ng_o[...] = rest[96:97, :][0]
     og_o[...] = jnp.concatenate([rest[104:105, :], rest[112:113, :]], axis=1)[0]
     lines = jnp.concatenate([rest[120:128, :], rest[128:136, :]], axis=1)
-    skip_o[...] = mm3(lines, pick_all(0), NT)[0, 0:HEADS]
+    skip_o[...] = mm3(jnp.concatenate([lines, lines], axis=0), pick_all(0), NT)[0, 0:HEADS]
     both = jnp.concatenate([rest[48:96, 0:128], jnp.zeros((80, 128), F32)], axis=0).T
     dtb_o[...] = both[0, 0 : 2 * HEADS]
     rate_o[...] = both[1, 0 : 2 * HEADS]
@@ -1076,7 +1076,7 @@
         middle_kernel,
         grid=(blocks,),
         in_specs=[
-            by_block((C, INNER)), by_block((C, D)), by_block((C, D)), by_block((C, D)),
+            by_block((C, INNER)), whole((count, D)), by_block((C, D)), whole((count, D)),
             by_block((1, C, 128)), by_block((C, GC)), by_block((1, 2, STATE, INNER)),
             whole((INNER, D)), whole((INNER, D)), whole((INNER,)),
         ],
@@ -1090,6 +1090,7 @@
             struct((blocks, 2, STATE, INNER)), struct((count, 128)), struct((blocks, C, 128)),
             struct((8, INNER)), struct((2 * INNER, D)),
         ],
+        scratch_shapes=[pltpu.VMEM((count, INNER), BF16), pltpu.VMEM((count, INNER), BF16)],
         compiler_params=pltpu.CompilerParams(dimension_semantics=dims, **params),
         name="middle",
     )(y, rounded, tok, cot, q, xact, sin, weight, out_weight, out_gain)

time: 344 us -> 312 us (0.907)
  Pallas kernels: 340 us -> 310 us
    pallas_call x1, Pallas kernels: 209 us -> 184 us  [on_device(): pl.pallas_call(lambda *refs: back_kernel(n, rows, length, far, shared, *r...]
    pallas_call x1, Pallas kernels: 78.1 us -> 72.4 us  [on_device(): pl.pallas_call(lambda *refs: front_kernel(n, rows, length, docs, *refs),...]
where the time goes in v3:
time: 312 us
  Pallas kernels  310 us (99%)
    pallas_call x1, Pallas kernels, on_device(): pl.pallas_call(lambda *refs: back_kernel(n, rows, length, far, shared, *r...  184 us
    pallas_call x1, Pallas kernels, on_device(): pl.pallas_call(lambda *refs: front_kernel(n, rows, length, docs, *refs),...  72.4 us
    pallas_call x1, Pallas kernels, on_device(): pl.pallas_call(middle_kernel, grid=(blocks,), in_specs=[by_block((C, INNE...  41.9 us
    pallas_call x1, Pallas kernels, on_device(): pl.pallas_call(finish_kernel, in_specs=[anywhere], out_specs=[anywhere, a...  11.8 us

profile of v3, /device:TPU:0, one launch (start us, length us, event | category | flops | bytes accessed | tf_op | source)
XLA Modules:
  0.0 312.2 jit_solution(14892491429250657269)
XLA Ops:
  0.6 72.4 %front.1 = (bf16[1024,768]{1,0:T(8,128)(2,1)}, f32[1024,1792]{1,0:T(8,128)}, f32[2,528,1792]{2,1,0:T(8,128)}, f32[1024,256]{1,0:T(8,128)}, f32[1024,1536]{1,0:T(...) custom-call(bf16[1024,768]{1,0:T(8,128)(2,1)} %bitcast.11, ...), custom_call_target="tpu_custom_call" | custom-call | tf_op jit(solution)/shard_map/front/pallas_call | solution.py:1029
  73.1 41.9 %middle.1 = (bf16[1024,768]{1,0:T(8,128)(2,1)}, f32[1024,1536]{1,0:T(8,128)}, f32[1024,768]{1,0:T(8,128)}, f32[4,2,64,1536]{3,2,1,0:T(8,128)}, f32[1024,128]{1,0...) custom-call(f32[1024,1536]{1,0:T(8,128)} %get-tuple-element.42.y, ...), custom_call_target="tpu_custom_call" | custom-call | tf_op jit(solution)/shard_map/middle/pallas_call | solution.py:1075
  115.0 184.3 %back.1 = (bf16[1024,768]{1,0:T(8,128)(2,1)}, f32[5120,768]{1,0:T(8,128)}) custom-call(f32[1024,1792]{1,0:T(8,128)} %get-tuple-element.48.refs_0_, f32[1024,1536]{1,0:T(8,128)} %get-tuple-element.49.refs_1_, f32[2,528,1792]{2,1,0:T(8,128)} %get-tuple-element.50.refs_2_, f32[4,1792]{1,0:T(4,128)} %refs_3_.1, bf16[3376,768]{1,0:T(8,128)(2,1)} %bitcast.9, ...), custom_call_target="tpu_custom_call" | custom-call | tf_op jit(solution)/shard_map/back/pallas_call | solution.py:1115
  299.3 0.0 copy-start
  299.3 11.8 %finish.1 = (f32[3376,768]{1,0:T(8,128)}, f32[1536,768]{1,0:T(8,128)}, f32[768]{0:T(1024)}, f32[4,1792]{1,0:T(4,128)}, f32[1792]{0:T(1024)}, /*index=5*/f32[48]{...) custom-call(f32[5120,768]{1,0:T(8,128)} %get-tuple-element.63.total), custom_call_target="tpu_custom_call" | custom-call | tf_op jit(solution)/shard_map/finish/pallas_call | solution.py:1160
  311.1 0.0 copy-done
  311.1 1.1 copy.24
Async XLA Ops:
  299.3 11.8 %copy-start = (bf16[1024,768]{1,0:T(8,128)(2,1)S(1)}, bf16[1024,768]{1,0:T(8,128)(2,1)}, u32[]{:S(2)}) copy-start(bf16[1024,768]{1,0:T(8,128)(2,1)} %get-tuple-element.62) | copy-start | bytes 4718596

commit v4 on v3

--- a/solution.py
+++ b/solution.py
@@ -240,7 +240,7 @@
 class Reduce:
     STAGES = 8
     SPACE = 2
-    LAG = 5
+    SLOTS, LAG = 15, 2
 
     def __init__(self, far, near_count, half, near, out, scratch):
         self.far, self.near_count, self.half, self.near, self.out = far, near_count, half, near, out
@@ -249,14 +249,14 @@
         self.y, self.core, self.z, self.x = rows // 2, rows % 2, seq // 2, seq % 2
 
     @staticmethod
-    def scratch(far):
+    def scratch():
         def slot(*shape):
             return pltpu.VMEM(shape + (D,), F32)
 
-        dma = pltpu.SemaphoreType.DMA
+        dma, count = pltpu.SemaphoreType.DMA, Reduce.SLOTS
         return [
-            slot(2, 128), slot(far, 128), slot(far, 64), slot(far, 32), slot(far, 24),
-            dma((12, far)), dma((12, far)), dma((2, far)),
+            slot(3, 128), slot(count, 128), slot(count, 64), slot(count, 32), slot(count, 24),
+            dma((12, count)), dma((12, count)), dma((2, count)),
         ]
 
     def device(self, x, y, z, core):
@@ -286,7 +286,7 @@
         return lax.rem(p, 2) == 1
 
     def slot(self, p):
-        return jnp.where(p < self.far, p, p - self.far)
+        return jnp.where(p < self.SLOTS, p, p - self.SLOTS)
 
     def places(self, p):
         x_first = self.turn(p)
@@ -344,7 +344,7 @@
 
     def own_in(self, p):
         return pltpu.make_async_copy(
-            self.half(p, self.core), self.own.at[lax.rem(p, 2)], self.local.at[0, self.slot(p)])
+            self.half(p, self.core), self.own.at[lax.rem(p, 3)], self.local.at[0, self.slot(p)])
 
     def own_out(self, p):
         i, start = self.slot(p), pl.multiple_of(self.places(p)[2], 8)
@@ -370,7 +370,7 @@
         def _():
             self.core_copy(p, False).wait()
             self.own_in(p).wait()
-            self.r0[i] += self.own[lax.rem(p, 2)]
+            self.r0[i] += self.own[lax.rem(p, 3)]
 
         @pl.when(p >= self.far)
         def _():
@@ -413,11 +413,11 @@
         return self.far + self.near_count + self.LAG + self.SPACE * self.STAGES
 
     def tick(self, t):
-        for s in range(self.STAGES, -1, -1):
+        for s in range(self.STAGES + 1):
             q = t - self.SPACE * s
-            p = jnp.where(q < self.far, q, q - self.LAG)
+            p = jnp.where(q < self.SLOTS, q, q - self.LAG)
             due = jnp.logical_and(q >= 0, p < self.far + self.near_count)
-            due = jnp.logical_and(due, jnp.logical_or(q < self.far, p >= self.far))
+            due = jnp.logical_and(due, jnp.logical_or(q < self.SLOTS, p >= self.SLOTS))
 
             @pl.when(due)
             def _(s=s, p=p):
@@ -431,7 +431,7 @@
     return [x[:, i * STATE : (i + 1) * STATE] for i in range(4)]
 
 
-START, GAP = 2, 1
+START, GAP = 4, 1
 
 
 def front_kernel(
@@ -620,7 +620,8 @@
     rd_f, rd_r = x[:, 2 * STATE : 3 * STATE], x[:, 3 * STATE :]
     s_f, s_r = sin[0, 0].astype(BF16), sin[0, 1].astype(BF16)
     pick_f, pick_r = pick_all(0), pick_all(2)
-    e_f, e_r = mm2(q[0], pick_f), mm2(q[0], pick_r)
+    factors = q[0].astype(BF16)
+    e_f, e_r = mm(factors, pick_f), mm(factors, pick_r)
     r_f, r_r = mm(rd_f, s_f), mm(rd_r, s_r)
     yv = y[...] + e_f * r_f + e_r * r_r
     gate = mm(rounded_b, wg[...], NT)
@@ -642,7 +643,7 @@
     dgates[here, :] = dgate
     drounded_o[...] = mm(dgate, wg[...])
     u_f, u_r = e_f * dy, e_r * dy
-    dq_o[0] = mm2(u_f * r_f, pick_f, NT) + mm2(u_r * r_r, pick_r, NT)
+    dq_o[0] = mm((u_f * r_f).astype(BF16), pick_f, NT) + mm((u_r * r_r).astype(BF16), pick_r, NT)
     u_f, u_r = u_f.astype(BF16), u_r.astype(BF16)
     ds_o[0, 1] = mm(rd_f, u_f, TN)
     ds_o[0, 0] = mm(rd_r, u_r, TN)
@@ -888,15 +889,6 @@
         st[G + 1, 0:48] = mm(draw[...], rounded[...])
         st[G + 1, 48:96, 0:128] = sums
 
-    def until(k):
-        return jnp.maximum(2 * (k - 2), 0)
-
-    if shared:
-
-        @pl.loop(jnp.where(k == 0, 0, until(k - 1)), until(k))
-        def _(t):
-            red.tick(t)
-
     @pl.when(k > far)
     def _():
         g = k - far - 1
@@ -921,6 +913,15 @@
         st[G + 1, pl.ds(line, 8), cols(lax.rem(g, 3))] = jnp.concatenate(
             taps + [bias, jnp.zeros((3, GC), F32)], axis=0)
         acc[...] += mm(both, w[...])
+
+    def until(k):
+        return jnp.clip(2 * (k - 2), 0, k + far + 1)
+
+    if shared:
+
+        @pl.loop(jnp.where(k == 0, 0, until(k - 1)), until(k))
+        def _(t):
+            red.tick(t)
 
     @pl.when(k == far + G + 1)
     def _():
@@ -1144,7 +1145,7 @@
             pltpu.VMEM((G + 1, rows, 8, GC), F32), pltpu.VMEM((G + 1, rows, 8, GC), F32),
             pltpu.SemaphoreType.DMA((3,)), pltpu.SemaphoreType.DMA((G + 1,)),
             pltpu.SemaphoreType.DMA((G + 1,)),
-            *Exchange.scratch(rows), *(Reduce.scratch(far_pieces) if shared else []),
+            *Exchange.scratch(rows), *(Reduce.scratch() if shared else []),
         ],
         compiler_params=pltpu.CompilerParams(
             dimension_semantics=dims, collective_id=1, has_side_effects=True,

time: 312 us -> 302 us (0.968)
  Pallas kernels: 310 us -> 300 us
    pallas_call x1, Pallas kernels: 72.4 us -> 67.8 us  [on_device(): pl.pallas_call(lambda *refs: front_kernel(n, rows, length, docs, *refs),...]
    pallas_call x1, Pallas kernels: 41.9 us -> 38.5 us  [on_device(): pl.pallas_call(middle_kernel, grid=(blocks,), in_specs=[by_block((C, INNE...]
where the time goes in v4:
time: 302 us
  Pallas kernels  300 us (99%)
    pallas_call x1, Pallas kernels, on_device(): pl.pallas_call(lambda *refs: back_kernel(n, rows, length, far, shared, *r...  182 us
    pallas_call x1, Pallas kernels, on_device(): pl.pallas_call(lambda *refs: front_kernel(n, rows, length, docs, *refs),...  67.8 us
    pallas_call x1, Pallas kernels, on_device(): pl.pallas_call(middle_kernel, grid=(blocks,), in_specs=[by_block((C, INNE...  38.5 us
    pallas_call x1, Pallas kernels, on_device(): pl.pallas_call(finish_kernel, in_specs=[anywhere], out_specs=[anywhere, a...  11.8 us

profile of v4, /device:TPU:0, one launch (start us, length us, event | category | flops | bytes accessed | tf_op | source)
XLA Modules:
  0.0 301.6 jit_solution(3010453807773479107)
XLA Ops:
  0.6 67.8 %front.1 = (bf16[1024,768]{1,0:T(8,128)(2,1)}, f32[1024,1792]{1,0:T(8,128)}, f32[2,528,1792]{2,1,0:T(8,128)}, f32[1024,256]{1,0:T(8,128)}, f32[1024,1536]{1,0:T(...) custom-call(bf16[1024,768]{1,0:T(8,128)(2,1)} %bitcast.11, ...), custom_call_target="tpu_custom_call" | custom-call | tf_op jit(solution)/shard_map/front/pallas_call | solution.py:1030
  68.4 38.5 %middle.1 = (bf16[1024,768]{1,0:T(8,128)(2,1)}, f32[1024,1536]{1,0:T(8,128)}, f32[1024,768]{1,0:T(8,128)}, f32[4,2,64,1536]{3,2,1,0:T(8,128)}, f32[1024,128]{1,0...) custom-call(f32[1024,1536]{1,0:T(8,128)} %get-tuple-element.42.y, ...), custom_call_target="tpu_custom_call" | custom-call | tf_op jit(solution)/shard_map/middle/pallas_call | solution.py:1076
  107.0 181.7 %back.1 = (bf16[1024,768]{1,0:T(8,128)(2,1)}, f32[5120,768]{1,0:T(8,128)}) custom-call(f32[1024,1792]{1,0:T(8,128)} %get-tuple-element.48.refs_0_, f32[1024,1536]{1,0:T(8,128)} %get-tuple-element.49.refs_1_, f32[2,528,1792]{2,1,0:T(8,128)} %get-tuple-element.50.refs_2_, f32[4,1792]{1,0:T(4,128)} %refs_3_.1, bf16[3376,768]{1,0:T(8,128)(2,1)} %bitcast.9, ...), custom_call_target="tpu_custom_call" | custom-call | tf_op jit(solution)/shard_map/back/pallas_call | solution.py:1116
  288.6 0.0 copy-start
  288.6 11.8 %finish.1 = (f32[3376,768]{1,0:T(8,128)}, f32[1536,768]{1,0:T(8,128)}, f32[768]{0:T(1024)}, f32[4,1792]{1,0:T(4,128)}, f32[1792]{0:T(1024)}, /*index=5*/f32[48]{...) custom-call(f32[5120,768]{1,0:T(8,128)} %get-tuple-element.63.total), custom_call_target="tpu_custom_call" | custom-call | tf_op jit(solution)/shard_map/finish/pallas_call | solution.py:1161
  300.4 0.0 copy-done
  300.5 1.1 copy.24
Async XLA Ops:
  288.6 11.8 %copy-start = (bf16[1024,768]{1,0:T(8,128)(2,1)S(1)}, bf16[1024,768]{1,0:T(8,128)(2,1)}, u32[]{:S(2)}) copy-start(bf16[1024,768]{1,0:T(8,128)(2,1)} %get-tuple-element.62) | copy-start | bytes 4718596

commit v5 on v4

--- a/solution.py
+++ b/solution.py
@@ -491,13 +491,13 @@
         ex.greet(True)
         for r in range(rows):
             hsend[r] = tok[(r + 1) * length - 16 : (r + 1) * length, :].astype(F32)[8:]
-        ex.met(True)
-        pl.when(ex.me < n - 1)(halo_copy().start)
         for r in range(rows):
             here = slice(r * length, (r + 1) * length)
             out = normed(tok[here, :].astype(F32))
             rext[r, PAD:, :] = out
             rounded_o[here, :] = out
+        ex.met(True)
+        pl.when(ex.me < n - 1)(halo_copy().start)
         dtb, rate = tall(dtb_i, 2 * HEADS).T[:48, 0:1], tall(rate_i, 2 * HEADS).T[:48, 0:1]
         lane = iota((48, 128), 1)
         tall_o[...] = jnp.where(lane == 0, dtb, jnp.where(lane == 1, rate, 0.0))
@@ -743,10 +743,6 @@
         ex.totals_of_passes()
         load_states().wait()
 
-        @pl.loop(0, G)
-        def _(g):
-            ex.totals(g)
-
         if shared:
             red.met()
         else:
@@ -755,6 +751,7 @@
 
         @pl.loop(0, G)
         def _(g):
+            ex.totals(g)
             ex.pair_copy(g).start()
 
         differ = iota((C, C), 0) != iota((C, C), 1)

time: 302 us -> 302 us (level)
  no operation moved by 1% of the time
where the time goes in v5:
time: 302 us
  Pallas kernels  300 us (99%)
    pallas_call x1, Pallas kernels, on_device(): pl.pallas_call(lambda *refs: back_kernel(n, rows, length, far, shared, *r...  182 us
    pallas_call x1, Pallas kernels, on_device(): pl.pallas_call(lambda *refs: front_kernel(n, rows, length, docs, *refs),...  67.3 us
    pallas_call x1, Pallas kernels, on_device(): pl.pallas_call(middle_kernel, grid=(blocks,), in_specs=[by_block((C, INNE...  38.5 us
    pallas_call x1, Pallas kernels, on_device(): pl.pallas_call(finish_kernel, in_specs=[anywhere], out_specs=[anywhere, a...  11.8 us

profile of v5, /device:TPU:0, one launch (start us, length us, event | category | flops | bytes accessed | tf_op | source)
XLA Modules:
  0.0 301.6 jit_solution(4754188939999121179)
XLA Ops:
  0.6 67.3 %front.1 = (bf16[1024,768]{1,0:T(8,128)(2,1)}, f32[1024,1792]{1,0:T(8,128)}, f32[2,528,1792]{2,1,0:T(8,128)}, f32[1024,256]{1,0:T(8,128)}, f32[1024,1536]{1,0:T(...) custom-call(bf16[1024,768]{1,0:T(8,128)(2,1)} %bitcast.11, ...), custom_call_target="tpu_custom_call" | custom-call | tf_op jit(solution)/shard_map/front/pallas_call | solution.py:1027
  68.0 38.5 %middle.1 = (bf16[1024,768]{1,0:T(8,128)(2,1)}, f32[1024,1536]{1,0:T(8,128)}, f32[1024,768]{1,0:T(8,128)}, f32[4,2,64,1536]{3,2,1,0:T(8,128)}, f32[1024,128]{1,0...) custom-call(f32[1024,1536]{1,0:T(8,128)} %get-tuple-element.42.y, ...), custom_call_target="tpu_custom_call" | custom-call | tf_op jit(solution)/shard_map/middle/pallas_call | solution.py:1073
  106.5 182.1 %back.1 = (bf16[1024,768]{1,0:T(8,128)(2,1)}, f32[5120,768]{1,0:T(8,128)}) custom-call(f32[1024,1792]{1,0:T(8,128)} %get-tuple-element.48.refs_0_, f32[1024,1536]{1,0:T(8,128)} %get-tuple-element.49.refs_1_, f32[2,528,1792]{2,1,0:T(8,128)} %get-tuple-element.50.refs_2_, f32[4,1792]{1,0:T(4,128)} %refs_3_.1, bf16[3376,768]{1,0:T(8,128)(2,1)} %bitcast.9, ...), custom_call_target="tpu_custom_call" | custom-call | tf_op jit(solution)/shard_map/back/pallas_call | solution.py:1113
  288.6 0.0 copy-start
  288.7 11.8 %finish.1 = (f32[3376,768]{1,0:T(8,128)}, f32[1536,768]{1,0:T(8,128)}, f32[768]{0:T(1024)}, f32[4,1792]{1,0:T(4,128)}, f32[1792]{0:T(1024)}, /*index=5*/f32[48]{...) custom-call(f32[5120,768]{1,0:T(8,128)} %get-tuple-element.63.total), custom_call_target="tpu_custom_call" | custom-call | tf_op jit(solution)/shard_map/finish/pallas_call | solution.py:1158
  300.5 0.0 copy-done
  300.5 1.1 copy.24
Async XLA Ops:
  288.6 11.8 %copy-start = (bf16[1024,768]{1,0:T(8,128)(2,1)S(1)}, bf16[1024,768]{1,0:T(8,128)(2,1)}, u32[]{:S(2)}) copy-start(bf16[1024,768]{1,0:T(8,128)(2,1)} %get-tuple-element.62) | copy-start | bytes 4718596
